TPU v7x, 32 devices: a whole 2x2x4 slice. The times are simulated.
32 devices in a mesh: fsdp: 8 (over z, x), seq: 4 (over y, core).
Axes of the slice: x: 2, y: 2, z: 4, core: 2. Of those that a mesh axis runs over, the one named last changes fastest.
Arguments:
- tokens: bfloat16 [8, 512, 3584], P('fsdp', 'seq'), may hold values from -6 to 6
- queries: bfloat16 [8, 512, 3584], P('fsdp', 'seq'), may hold values from -21 to 21
- cotangent: bfloat16 [8, 512, 3584], P('fsdp', 'seq'), may hold values from -6 to 6
- modality: int32 [8, 512], P('fsdp', 'seq'), may hold values from 0 to 1, as said below
- block_ids: int32 [8, 512], P('fsdp', 'seq'), may hold values from 0 to 511, as said below
- kv_weight: bfloat16 [2, 3584, 1024], P(None, 'fsdp', 'seq'), may hold values from -0.09375 to 0.09375
Outputs:
- attended: bfloat16 [8, 512, 3584], P('fsdp', 'seq')
- grad_queries: bfloat16 [8, 512, 3584], P('fsdp', 'seq')
- grad_tokens: bfloat16 [8, 512, 3584], P('fsdp', 'seq')
- grad_kv_weight: float32 [2, 3584, 1024], P(None, 'fsdp', 'seq')
Inputs may be any that keep to these rules, and one draw needn't show every extreme that they name: `modality`: the first 32 tokens of a sequence are text; video tokens come in whole frames of 32 tokens starting at multiples of 32. `block_ids`: a text token's id is its position in its sequence; a video token's id is the position of the last token of its frame.
All inputs are finite; a program needn't handle non-finite values.
Results may differ from a plain program's by a relative error of at most 0.015.
The roundings to bfloat16 on the way count: a program that leaves them out, or rounds other values in their place, can miss the bound.
Values may be sent and summed in bfloat16 or wider, within the bound.
No kernel may reach another device: no remote copies, remote signals or barrier semaphores. Data moves between devices by JAX's collectives and lax.ppermute only.
A program may use at most 128 MiB of HBM per device.

v0:
```python
import functools

import jax
import jax.numpy as jnp
from jax import lax
from jax.experimental import pallas as pl
from jax.experimental.pallas import tpu as pltpu
from jax.sharding import PartitionSpec as P

HEAD_DIM = 128
GROUP = 7
SCALE = HEAD_DIM ** (-0.5)
LOG2E = 1.4426950408889634
HIDDEN = -1e30
F32 = jnp.float32
BF16 = jnp.bfloat16


def contract(a, b, da, db):
    return lax.dot_general(a, b, (((da,), (db,)), ((), ())), preferred_element_type=F32)


def attend_kernel(count, heads_ref, q_ref, up_ref, *refs):
    kv_refs, (qb_ref, kb_ref) = refs[:count], refs[count : count + 2]
    att_ref, gq_ref, gkv_ref, bias, qs, ups, pbs, his, los = refs[-9:]
    rows = q_ref.shape[0]
    step = pl.program_id(0)

    @pl.when(step == 0)
    def _():
        bias[...] = jnp.where(kb_ref[...] <= qb_ref[...], 0.0, HIDDEN).astype(F32)

    kv = kv_refs[0][...]
    for r in range(1, count):
        kv = jnp.where(step == r, kv_refs[r][...], kv)
    keys = kv[:, :HEAD_DIM]
    values = kv[:, HEAD_DIM:]
    for h in range(GROUP):
        cols = slice(h * HEAD_DIM, (h + 1) * HEAD_DIM)
        here = slice(h * rows, (h + 1) * rows)
        q = q_ref[:, cols]
        up = up_ref[:, cols]
        scores = contract(q, keys, 1, 1) * (SCALE * LOG2E) + bias[...]
        expo = jnp.exp2(scores - jnp.max(scores, axis=-1, keepdims=True))
        probs = expo * (1.0 / jnp.sum(expo, axis=-1, keepdims=True))
        pb = probs.astype(BF16)
        att_ref[:, cols] = contract(pb, values, 1, 0).astype(BF16)
        dp = contract(up, values, 1, 1).astype(BF16).astype(F32)
        ds = probs * (dp - jnp.sum(probs * dp, axis=-1, keepdims=True))
        hi = ds.astype(BF16)
        lo = (ds - hi.astype(F32)).astype(BF16)
        gq_ref[:, cols] = ((contract(hi, keys, 1, 0) + contract(lo, keys, 1, 0)) * SCALE).astype(BF16)
        qs[here, :] = q
        ups[here, :] = up
        pbs[here, :] = pb
        his[here, :] = hi
        los[here, :] = lo
    dk = (contract(qs[...], his[...], 0, 0) + contract(qs[...], los[...], 0, 0)) * SCALE
    dv = contract(ups[...], pbs[...], 0, 0)
    gkv_ref[0, :, :HEAD_DIM] = dk.T
    gkv_ref[0, :, HEAD_DIM:] = dv.T


def attend(heads, queries, upstream, kvs, query_blocks, key_blocks, before=()):
    rows, width = queries.shape
    length, pair = kvs[0].shape
    count = len(kvs)
    span = GROUP * HEAD_DIM
    by_head = pl.BlockSpec((rows, span), lambda r, heads: (0, heads[r]))
    whole = pl.BlockSpec((length, pair), lambda r, heads: (0, 0))
    stacked = (GROUP * rows, length)
    return pl.pallas_call(
        functools.partial(attend_kernel, count),
        grid_spec=pltpu.PrefetchScalarGridSpec(
            num_scalar_prefetch=1,
            grid=(count,),
            in_specs=[by_head, by_head]
            + [whole] * count
            + [
                pl.BlockSpec((rows, 1), lambda r, heads: (0, 0)),
                pl.BlockSpec((1, length), lambda r, heads: (0, 0)),
            ]
            + [pl.BlockSpec(memory_space=pl.ANY)] * len(before),
            out_specs=[
                by_head,
                by_head,
                pl.BlockSpec((1, length, pair), lambda r, heads: (r, 0, 0)),
            ],
            scratch_shapes=[
                pltpu.VMEM((rows, length), F32),
                pltpu.VMEM((GROUP * rows, HEAD_DIM), BF16),
                pltpu.VMEM((GROUP * rows, HEAD_DIM), BF16),
                pltpu.VMEM(stacked, BF16),
                pltpu.VMEM(stacked, BF16),
                pltpu.VMEM(stacked, BF16),
            ],
        ),
        out_shape=[
            jax.ShapeDtypeStruct((rows, width), BF16),
            jax.ShapeDtypeStruct((rows, width), BF16),
            jax.ShapeDtypeStruct((count, length, pair), F32),
        ],
        input_output_aliases={5 + count + i: i for i in range(len(before))},
        compiler_params=pltpu.CompilerParams(vmem_limit_bytes=32 * 1024 * 1024),
        cost_estimate=pl.CostEstimate(
            flops=2 * 7 * count * GROUP * rows * length * HEAD_DIM,
            bytes_accessed=8 * rows * count * span + 6 * count * length * pair,
            transcendentals=count * GROUP * rows * length,
        ),
    )(heads, queries, upstream, *kvs, query_blocks, key_blocks, *before)


def per_device(fsdp, seq, tokens, queries, cotangent, modality, block_ids, kv_weight):
    tokens, queries, cotangent = tokens[0], queries[0], cotangent[0]
    me_f = lax.axis_index("fsdp")
    me_s = lax.axis_index("seq")
    rows, width = tokens.shape
    depth, pair = kv_weight.shape[1:]
    length = seq * rows

    def swap(x, axis, bit):
        size = fsdp if axis == "fsdp" else seq
        return lax.ppermute(x, axis, [(i, i ^ bit) for i in range(size)])

    def over_seq(x):
        across = swap(x, "seq", 2)
        return [x, swap(x, "seq", 1), across, swap(across, "seq", 1)]

    def place(parts):
        whole = jnp.zeros((seq, *parts[0].shape), parts[0].dtype)
        for r, part in enumerate(parts):
            whole = lax.dynamic_update_index_in_dim(whole, part, me_s ^ r, 0)
        return whole

    def over_fsdp(x):
        if fsdp != 8:
            return lax.all_gather(x, "fsdp", axis=0)
        whole = jnp.zeros((fsdp, *x.shape), x.dtype)
        for step in range(4):
            owner = lax.rem(me_f + fsdp - 2 * step, fsdp)
            whole = lax.dynamic_update_index_in_dim(whole, x, owner, 0)
            whole = lax.dynamic_update_index_in_dim(whole, swap(x, "fsdp", 1), owner ^ 1, 0)
            if step < 3:
                x = lax.ppermute(x, "fsdp", [(i, (i + 2) % fsdp) for i in range(fsdp)])
        return whole

    def by_expert(kind, x):
        zero = jnp.zeros_like(x)
        return jnp.concatenate([jnp.where(kind == e, x, zero) for e in range(2)], axis=-1)

    both = jnp.concatenate([kv_weight[0], kv_weight[1]], axis=-1)
    weight = over_fsdp(both).reshape(width, 2 * pair)
    hidden = place(over_seq(tokens)).reshape(length, width)
    ids = place(over_seq(jnp.stack([modality[0], block_ids[0]])))
    modal_here = ids[:, 0].reshape(length, 1)
    blocks_here = ids[:, 1].reshape(1, length)

    parts = jnp.dot(hidden, weight, preferred_element_type=F32)
    key_value = jnp.where(modal_here == 1, parts[:, pair:], parts[:, :pair]).astype(BF16)

    kvs = over_seq(key_value)
    heads = me_s ^ jnp.arange(seq, dtype=jnp.int32)
    query_blocks = block_ids[0][:, None]
    out_a, out_q, far = attend(heads[2:], queries, cotangent, kvs[2:], query_blocks, blocks_here)
    attended, grad_queries, near = attend(
        heads[:2], queries, cotangent, kvs[:2], query_blocks, blocks_here, (out_a, out_q)
    )
    arriving = swap(far[0] + swap(far[1], "seq", 1), "seq", 2)
    grad_kv = (near[0] + swap(near[1], "seq", 1) + arriving).astype(BF16)

    lanes = -(-(depth + 1) // 128) * 128
    columns = tokens.reshape(rows, fsdp, depth).transpose(1, 0, 2)
    kinds = jnp.broadcast_to(modality[0].astype(BF16)[None, :, None], (fsdp, rows, 1))
    blank = jnp.zeros((fsdp, rows, lanes - depth - 1), BF16)
    columns = jnp.concatenate([columns, kinds, blank], axis=-1)
    columns = lax.all_to_all(columns, "fsdp", split_axis=0, concat_axis=0, tiled=True)
    columns = over_seq(columns)

    all_grad = over_fsdp(grad_kv)
    total = 0.0
    for r, part in enumerate(columns):
        quarter = lax.dynamic_slice_in_dim(all_grad, (me_s ^ r) * rows, rows, 1).reshape(fsdp * rows, pair)
        part = part.reshape(fsdp * rows, lanes)
        total = total + contract(part, by_expert(part[:, depth : depth + 1], quarter), 0, 0)
    grad_weight = jnp.stack([total[:depth, :pair], total[:depth, pair:]])

    weight_c = swap(weight, "seq", 1)
    grad_c = swap(grad_kv, "seq", 1)

    def hidden_grad(quarter):
        kind = lax.dynamic_slice_in_dim(modal_here, quarter * rows, rows)
        total = 0.0
        for g, w in ((grad_kv, weight), (grad_c, weight_c)):
            g = lax.dynamic_slice_in_dim(g, quarter * rows, rows)
            total = total + contract(by_expert(kind, g), w, 1, 1)
        return total

    away = swap(hidden_grad(me_s ^ 2).astype(BF16), "seq", 2)
    grad_tokens = (hidden_grad(me_s) + away.astype(F32)).astype(BF16)
    return attended[None], grad_queries[None], grad_tokens[None], grad_weight


def solution(mesh):
    split = P("fsdp", "seq", None)
    weights = P(None, "fsdp", "seq")
    return jax.shard_map(
        functools.partial(per_device, mesh.shape["fsdp"], mesh.shape["seq"]),
        mesh=mesh,
        in_specs=(split, split, split, P("fsdp", "seq"), P("fsdp", "seq"), weights),
        out_specs=(split, split, split, weights),
        check_vma=False,
    )
```

profile of v0, /device:TPU:0, one launch (start us, length us, event | category | flops | bytes accessed | tf_op | source)
XLA Modules:
  0.0 212.5 jit_solution(13401547816121936571)
XLA Ops:
  0.6 1.1 slice_bitcast_fusion.5
  2.5 2.9 %collective-permute-start.6 = (bf16[448,512]{1,0:T(8,128)(2,1)}, bf16[448,512]{1,0:T(8,128)(2,1)}, u32[]{:S(2)}, u32[]{:S(2)}) collective-permute-start(bf16[448,512]{1,0:T(8,128)(2,1)} %pad_maximum_fusion.1), channel_id=1, source_target_pairs={{0,4},{4,0},{8,12},{12,8},{16,20},{20,16},{24,28},{28,24},{1,5},{5... | collective-permute-start | bytes 1376264 | tf_op jit(solution)/shard_map/ppermute | solution.py:123
  5.5 1.6 collective-permute-start.7
  7.1 1.5 collective-permute-start.4
  9.5 1.5 copy.24
  11.2 1.2 maximum_maximum_fusion
  12.4 4.2 %all-to-all-start = ((bf16[8,128,512]{1,2,0:T(8,128)(2,1)}), bf16[8,128,512]{1,2,0:T(8,128)(2,1)}, u32[]{:S(2)}, u32[]{:S(2)}) async-start(bf16[8,128,512]{1,2,0:T(8,128)(2,1)} %maximum_maximum_fusion), calls=%async_computation | async-start | bytes 2097152 | tf_op jit(solution)/shard_map/all_to_all | solution.py:176
  16.7 2.1 broadcast_in_dim.220
  19.7 2.1 broadcast_in_dim.224
  23.2 6.9 %collective-permute-done.1 = s32[2,128]{1,0:T(2,128)S(1)} collective-permute-done((s32[2,128]{1,0:T(2,128)S(1)}, s32[2,128]{1,0:T(2,128)S(1)}, u32[]{:S(2)}, u32[]{:S(2)}) %collective-permute-start.1) | collective-permute-done | bytes 1056 | tf_op jit(solution)/shard_map/ppermute | solution.py:123
  31.9 1.6 collective-permute-start.9
  33.4 1.8 bitcast_dynamic-update-slice_fusion.9
  35.3 1.8 bitcast_dynamic-update-slice_fusion.8
  37.1 11.2 %collective-permute-done.9 = bf16[448,512]{1,0:T(8,128)(2,1)S(1)} collective-permute-done((bf16[448,512]{1,0:T(8,128)(2,1)}, bf16[448,512]{1,0:T(8,128)(2,1)S(1)}, u32[]{:S(2)}, u32[]{:S(2)}) %collective-permute-start.9) | collective-permute-done | bytes 458784 | tf_op jit(solution)/shard_map/ppermute | solution.py:144
  48.3 1.5 collective-permute-start.10
  49.8 3.4 %collective-permute-start.11 = (bf16[448,512]{1,0:T(8,128)(2,1)S(1)}, bf16[448,512]{1,0:T(8,128)(2,1)S(1)}, u32[]{:S(2)}, u32[]{:S(2)}) collective-permute-start(bf16[448,512]{1,0:T(8,128)(2,1)S(1)} %collective-permute-done.9), channel_id=1, source_target_pairs={{0,8},{4,12},{8,16},{12,20},{16,24},{20,28},{24,0},{28,4},{1,9},{5... | collective-permute-start | bytes 1376264 | tf_op jit(solution)/shard_map/ppermute | solution.py:144
  53.2 2.2 %bitcast_dynamic-update-slice_fusion.2 = bf16[4,128,3584]{2,1,0:T(8,128)(2,1)} fusion(bf16[4,128,3584]{2,1,0:T(8,128)(2,1)} %constant_dynamic-update-slice_fusion, s32[]{:T(128)S(6)} %select_n.125, bf16[128,3584]{1,0:T(8,128)(2,1)} %collective-permute-done.3), kind=kLoop, calls=%fused_computation.26 | loop fusion | bytes 1835012 | tf_op jit(solution)/shard_map/jit(dynamic_update_index_in_dim)/dynamic_update_slice | solution.py:132
  57.9 5.3 %collective-permute-done.11 = bf16[448,512]{1,0:T(8,128)(2,1)S(1)} collective-permute-done((bf16[448,512]{1,0:T(8,128)(2,1)S(1)}, bf16[448,512]{1,0:T(8,128)(2,1)S(1)}, u32[]{:S(2)}, u32[]{:S(2)}) %collective-permute-start.11) | collective-permute-done | bytes 458784 | tf_op jit(solution)/shard_map/ppermute | solution.py:144
  66.9 7.3 %collective-permute-done.12 = bf16[448,512]{1,0:T(8,128)(2,1)S(1)} collective-permute-done((bf16[448,512]{1,0:T(8,128)(2,1)S(1)}, bf16[448,512]{1,0:T(8,128)(2,1)S(1)}, u32[]{:S(2)}, u32[]{:S(2)}) %collective-permute-start.12) | collective-permute-done | bytes 458784 | tf_op jit(solution)/shard_map/ppermute | solution.py:123
  75.0 5.3 %fusion.45 = bf16[512,512]{1,0:T(8,128)(2,1)S(1)} fusion(bf16[512,3584]{1,0:T(8,128)(2,1)} %bitcast.15, bf16[3584,512]{1,0:T(8,128)(2,1)} %bitcast.26), kind=kOutput, calls=%fused_computation.119 | convolution fusion | flops 1879048192 | bytes 7864320 | tf_op jit(solution)/shard_map/dot_general | solution.py:158
  81.1 5.9 %collective-permute-done.14.refs_0_ = bf16[512,256]{1,0:T(8,128)(2,1)S(1)} collective-permute-done((bf16[512,256]{1,0:T(8,128)(2,1)S(1)}, bf16[512,256]{1,0:T(8,128)(2,1)S(1)}, u32[]{:S(2)}, u32[]{:S(2)}) %collective-permute-start.14) | collective-permute-done | bytes 262176 | tf_op jit(solution)/shard_map/ppermute | solution.py:123
  91.1 11.4 %shard_map.93 = (bf16[128,3584]{1,0:T(8,128)(2,1)}, bf16[128,3584]{1,0:T(8,128)(2,1)}, f32[2,512,256]{2,1,0:T(8,128)S(1)}) custom-call(s32[2]{0:T(128)S(1)} %get-tuple-element.60.heads_ref, bf16[128,3584]{1,0:T(8,128)(2,1)S(1)} %bitcast.126, bf16[128,3584]{1,0:T(8,128)(2,1)S(1)} %bitcast.128, bf16[512,256]{1,0:T(8,128)(2,1)S(1)} %copy-done.4, ...), custom_call_target="tpu_custom_call" | custom-call | flops 1644167168 | bytes 3407872 | tf_op jit(solution)/shard_map/pallas_call | solution.py:72
  104.0 1.2 copy-done.2
  105.2 12.3 %shard_map.94 = (bf16[128,3584]{1,0:T(8,128)(2,1)}, bf16[128,3584]{1,0:T(8,128)(2,1)}, f32[2,512,256]{2,1,0:T(8,128)S(1)}) custom-call(s32[2]{0:T(128)S(1)} %get-tuple-element.61.heads_ref, bf16[128,3584]{1,0:T(8,128)(2,1)S(1)} %bitcast.127, bf16[128,3584]{1,0:T(8,128)(2,1)S(1)} %bitcast.129, ...), custom_call_target="tpu_custom_call", output_to_operand_aliasing={{0}: (7, {}), {1}: (8, {})} | custom-call | flops 1644167168 | bytes 3407872 | tf_op jit(solution)/shard_map/pallas_call | solution.py:72
  118.8 1.9 bitcast_add_fusion
  120.7 1.5 collective-permute-start.18
  122.8 1.5 copy.25
  124.7 5.0 %collective-permute-done.30 = bf16[8,128,512]{1,2,0:T(8,128)(2,1)} collective-permute-done((bf16[8,128,512]{1,2,0:T(8,128)(2,1)}, bf16[8,128,512]{1,2,0:T(8,128)(2,1)}, u32[]{:S(2)}, u32[]{:S(2)}) %collective-permute-start.30) | collective-permute-done | bytes 1048608 | tf_op jit(solution)/shard_map/ppermute | solution.py:123
  129.7 2.3 %copy.27 = bf16[8,128,512]{2,1,0:T(8,128)(2,1)} copy(bf16[8,128,512]{1,2,0:T(8,128)(2,1)} %collective-permute-done.30) | data formatting | bytes 2097152 | tf_op jit(solution)/shard_map/ppermute | solution.py:123
  132.0 2.3 %copy.26 = bf16[8,128,512]{2,1,0:T(8,128)(2,1)} copy(bf16[8,128,512]{1,2,0:T(8,128)(2,1)} %collective-permute-done.29) | data formatting | bytes 2097152 | tf_op jit(solution)/shard_map/ppermute | solution.py:123
  134.3 6.1 %collective-permute-done.18 = f32[512,256]{1,0:T(8,128)} collective-permute-done((f32[512,256]{1,0:T(8,128)}, f32[512,256]{1,0:T(8,128)}, u32[]{:S(2)}, u32[]{:S(2)}) %collective-permute-start.18) | collective-permute-done | bytes 524320 | tf_op jit(solution)/shard_map/ppermute | solution.py:123
  140.6 1.3 bitcast_dynamic-update-slice_fusion.18
  141.8 1.5 collective-permute-start.22
  143.3 2.4 %collective-permute-start.23 = (bf16[512,256]{1,0:T(8,128)(2,1)S(1)}, bf16[512,256]{1,0:T(8,128)(2,1)}, u32[]{:S(2)}, u32[]{:S(2)}) collective-permute-start(bf16[512,256]{1,0:T(8,128)(2,1)S(1)} %get-tuple-element.25), channel_id=1, source_target_pairs={{0,8},{4,12},{8,16},{12,20},{16,24},{20,28},{24,0},{28,4},{1,9},{5... | collective-permute-start | bytes 786440 | tf_op jit(solution)/shard_map/ppermute | solution.py:144
  145.8 1.4 compare_reduce_fusion.5
  147.1 1.9 compare_reduce_fusion.3
  149.1 4.5 %collective-permute-done.23 = bf16[512,256]{1,0:T(8,128)(2,1)} collective-permute-done((bf16[512,256]{1,0:T(8,128)(2,1)S(1)}, bf16[512,256]{1,0:T(8,128)(2,1)}, u32[]{:S(2)}, u32[]{:S(2)}) %collective-permute-start.23) | collective-permute-done | bytes 262176 | tf_op jit(solution)/shard_map/ppermute | solution.py:144
  155.3 1.4 broadcast_select_fusion.2
  156.7 6.2 %collective-permute-done.25 = bf16[512,256]{1,0:T(8,128)(2,1)} collective-permute-done((bf16[512,256]{1,0:T(8,128)(2,1)}, bf16[512,256]{1,0:T(8,128)(2,1)}, u32[]{:S(2)}, u32[]{:S(2)}) %collective-permute-start.25) | collective-permute-done | bytes 262176 | tf_op jit(solution)/shard_map/ppermute | solution.py:144
  162.9 1.4 collective-permute-start.26
  164.3 1.5 copy.28
  168.2 4.6 %collective-permute-done.27 = bf16[512,256]{1,0:T(8,128)(2,1)} collective-permute-done((bf16[512,256]{1,0:T(8,128)(2,1)}, bf16[512,256]{1,0:T(8,128)(2,1)}, u32[]{:S(2)}, u32[]{:S(2)}) %collective-permute-start.27) | collective-permute-done | bytes 262176 | tf_op jit(solution)/shard_map/ppermute | solution.py:144
  175.4 4.0 %collective-permute-done.28 = bf16[512,256]{1,0:T(8,128)(2,1)S(1)} collective-permute-done((bf16[512,256]{1,0:T(8,128)(2,1)}, bf16[512,256]{1,0:T(8,128)(2,1)S(1)}, u32[]{:S(2)}, u32[]{:S(2)}) %collective-permute-start.28) | collective-permute-done | bytes 262176 | tf_op jit(solution)/shard_map/ppermute | solution.py:123
  184.3 3.3 %fusion.30 = f32[128,3584]{1,0:T(8,128)S(1)} fusion(bf16[3584,512]{1,0:T(8,128)(2,1)} %collective-permute-done.20, bf16[128,256]{1,0:T(8,128)(2,1)S(1)} %copy-done.13, bf16[128,256]{1,0:T(8,128)(2,1)S(1)} %copy-done.12), kind=kOutput, calls=%fused_computation.82 | convolution fusion | flops 470024192 | bytes 5636096 | tf_op jit(solution)/shard_map/dot_general | solution.py:20
  187.7 3.4 %fusion.2 = bf16[128,3584]{1,0:T(8,128)(2,1)S(1)} fusion(f32[128,3584]{1,0:T(8,128)S(1)} %fusion.30, bf16[3584,512]{1,0:T(8,128)(2,1)} %bitcast.26, bf16[128,256]{1,0:T(8,128)(2,1)S(1)} %get-tuple-element.54, bf16[128,256]{1,0:T(8,128)(2,1)S(1)} %get-tuple-element.52), kind=kOutput, calls=%fused_computation.4 | convolution fusion | flops 470941696 | bytes 6553600 | tf_op jit(solution)/shard_map/dot_general | solution.py:20
  193.2 3.3 %fusion.23 = f32[128,3584]{1,0:T(8,128)S(1)} fusion(bf16[3584,512]{1,0:T(8,128)(2,1)} %collective-permute-done.20, bf16[128,256]{1,0:T(8,128)(2,1)S(1)} %get-tuple-element.47, bf16[128,256]{1,0:T(8,128)(2,1)S(1)} %get-tuple-element.49), kind=kOutput, calls=%fused_computation.75 | convolution fusion | flops 470024192 | bytes 5636096 | tf_op jit(solution)/shard_map/dot_general | solution.py:20
  196.6 11.7 %collective-permute-done.21 = bf16[128,3584]{1,0:T(8,128)(2,1)S(1)} collective-permute-done((bf16[128,3584]{1,0:T(8,128)(2,1)S(1)}, bf16[128,3584]{1,0:T(8,128)(2,1)S(1)}, u32[]{:S(2)}, u32[]{:S(2)}) %collective-permute-start.21) | collective-permute-done | bytes 917536 | tf_op jit(solution)/shard_map/ppermute | solution.py:123
  208.2 4.3 %fusion.3 = bf16[1,128,3584]{2,1,0:T(8,128)(2,1)} fusion(f32[128,3584]{1,0:T(8,128)S(1)} %fusion.23, bf16[3584,512]{1,0:T(8,128)(2,1)} %bitcast.26, bf16[128,3584]{1,0:T(8,128)(2,1)S(1)} %collective-permute-done.21, bf16[128,256]{1,0:T(8,128)(2,1)S(1)} %get-tuple-element.53, bf16[128,256]{1,0:T(8,128)(2,1)S(1)} %get-tuple-element.55), kind=kOutput, calls=%fused_computation.5 | convolution fusion | flops 471859200 | bytes 7471104 | tf_op jit(solution)/shard_map/dot_general | solution.py:20
  (127 shorter events, 35.5 us)
Async XLA Ops:
  0.6 10.4 %copy-start.17 = (s32[1,128]{1,0:T(1,128)S(1)}, s32[1,128]{1,0:T(1,128)}, u32[]{:S(2)}) copy-start(s32[1,128]{1,0:T(1,128)} %param.9) | copy-start | bytes 1540
  2.5 30.9 %collective-permute-start.6 = (bf16[448,512]{1,0:T(8,128)(2,1)}, bf16[448,512]{1,0:T(8,128)(2,1)}, u32[]{:S(2)}, u32[]{:S(2)}) collective-permute-start(bf16[448,512]{1,0:T(8,128)(2,1)} %pad_maximum_fusion.1), channel_id=1, source_target_pairs={{0,4},{4,0},{8,12},{12,8},{16,20},{20,16},{24,28},{28,24},{1,5},{5... | collective-permute-start | bytes 1376264 | tf_op jit(solution)/shard_map/ppermute | solution.py:123
  5.5 25.8 %collective-permute-start.7 = (bf16[448,512]{1,0:T(8,128)(2,1)}, bf16[448,512]{1,0:T(8,128)(2,1)}, u32[]{:S(2)}, u32[]{:S(2)}) collective-permute-start(bf16[448,512]{1,0:T(8,128)(2,1)} %pad_maximum_fusion.1), channel_id=1, source_target_pairs={{0,8},{4,12},{8,16},{12,20},{16,24},{20,28},{24,0},{28,4},{1,9},{5... | collective-permute-start | bytes 1376264 | tf_op jit(solution)/shard_map/ppermute | solution.py:144
  7.0 46.1 %collective-permute-start.3 = (bf16[128,3584]{1,0:T(8,128)(2,1)}, bf16[128,3584]{1,0:T(8,128)(2,1)}, u32[]{:S(2)}, u32[]{:S(2)}) collective-permute-start(bf16[128,3584]{1,0:T(8,128)(2,1)} %bitcast.131), channel_id=1, source_target_pairs={{0,1},{1,0},{2,3},{3,2},{4,5},{5,4},{6,7},{7,6},{8,9},{9,8},{10,11... | collective-permute-start | bytes 2752520 | tf_op jit(solution)/shard_map/ppermute | solution.py:123
  7.1 46.1 %collective-permute-start.4 = (bf16[128,3584]{1,0:T(8,128)(2,1)}, bf16[128,3584]{1,0:T(8,128)(2,1)S(1)}, u32[]{:S(2)}, u32[]{:S(2)}) collective-permute-start(bf16[128,3584]{1,0:T(8,128)(2,1)} %bitcast.132), channel_id=1, source_target_pairs={{0,2},{1,3},{2,0},{3,1},{4,6},{5,7},{6,4},{7,5},{8,10},{9,11},{10,... | collective-permute-start | bytes 2752520 | tf_op jit(solution)/shard_map/ppermute | solution.py:123
  9.3 13.4 %collective-permute-start = (s32[2,128]{1,0:T(2,128)S(1)}, s32[2,128]{1,0:T(2,128)S(1)}, u32[]{:S(2)}, u32[]{:S(2)}) collective-permute-start(s32[2,128]{1,0:T(2,128)S(1)} %pad_add_fusion), channel_id=1, source_target_pairs={{0,1},{1,0},{2,3},{3,2},{4,5},{5,4},{6,7},{7,6},{8,9},{9,8},{10,11... | collective-permute-start | bytes 3080 | tf_op jit(solution)/shard_map/ppermute | solution.py:123
  11.2 7.6 %copy-start.7 = (bf16[1,128,3584]{2,1,0:T(8,128)(2,1)S(1)}, bf16[1,128,3584]{2,1,0:T(8,128)(2,1)}, u32[]{:S(2)}) copy-start(bf16[1,128,3584]{2,1,0:T(8,128)(2,1)} %param.6) | copy-start | bytes 2752516
  12.4 91.0 %all-to-all-start = ((bf16[8,128,512]{1,2,0:T(8,128)(2,1)}), bf16[8,128,512]{1,2,0:T(8,128)(2,1)}, u32[]{:S(2)}, u32[]{:S(2)}) async-start(bf16[8,128,512]{1,2,0:T(8,128)(2,1)} %maximum_maximum_fusion), calls=%async_computation | async-start | bytes 2097152 | tf_op jit(solution)/shard_map/all_to_all | solution.py:176
  22.7 7.4 %collective-permute-start.1 = (s32[2,128]{1,0:T(2,128)S(1)}, s32[2,128]{1,0:T(2,128)S(1)}, u32[]{:S(2)}, u32[]{:S(2)}) collective-permute-start(s32[2,128]{1,0:T(2,128)S(1)} %pad_add_fusion), channel_id=1, source_target_pairs={{0,2},{1,3},{2,0},{3,1},{4,6},{5,7},{6,4},{7,5},{8,10},{9,11},{10,... | collective-permute-start | bytes 3080 | tf_op jit(solution)/shard_map/ppermute | solution.py:123
  30.1 1.1 collective-permute-start.2
  31.3 25.1 %collective-permute-start.8 = (bf16[448,512]{1,0:T(8,128)(2,1)}, bf16[448,512]{1,0:T(8,128)(2,1)S(1)}, u32[]{:S(2)}, u32[]{:S(2)}) collective-permute-start(bf16[448,512]{1,0:T(8,128)(2,1)} %collective-permute-done.7), channel_id=1, source_target_pairs={{0,4},{4,0},{8,12},{12,8},{16,20},{20,16},{24,28},{28,24},{1,5},{5... | collective-permute-start | bytes 1376264 | tf_op jit(solution)/shard_map/ppermute | solution.py:123
  31.9 16.5 %collective-permute-start.9 = (bf16[448,512]{1,0:T(8,128)(2,1)}, bf16[448,512]{1,0:T(8,128)(2,1)S(1)}, u32[]{:S(2)}, u32[]{:S(2)}) collective-permute-start(bf16[448,512]{1,0:T(8,128)(2,1)} %collective-permute-done.7), channel_id=1, source_target_pairs={{0,8},{4,12},{8,16},{12,20},{16,24},{20,28},{24,0},{28,4},{1,9},{5... | collective-permute-start | bytes 1376264 | tf_op jit(solution)/shard_map/ppermute | solution.py:144
  48.3 15.9 %collective-permute-start.10 = (bf16[448,512]{1,0:T(8,128)(2,1)S(1)}, bf16[448,512]{1,0:T(8,128)(2,1)S(1)}, u32[]{:S(2)}, u32[]{:S(2)}) collective-permute-start(bf16[448,512]{1,0:T(8,128)(2,1)S(1)} %collective-permute-done.9), channel_id=1, source_target_pairs={{0,4},{4,0},{8,12},{12,8},{16,20},{20,16},{24,28},{28,24},{1,5},{5... | collective-permute-start | bytes 1376264 | tf_op jit(solution)/shard_map/ppermute | solution.py:123
  49.8 13.5 %collective-permute-start.11 = (bf16[448,512]{1,0:T(8,128)(2,1)S(1)}, bf16[448,512]{1,0:T(8,128)(2,1)S(1)}, u32[]{:S(2)}, u32[]{:S(2)}) collective-permute-start(bf16[448,512]{1,0:T(8,128)(2,1)S(1)} %collective-permute-done.9), channel_id=1, source_target_pairs={{0,8},{4,12},{8,16},{12,20},{16,24},{20,28},{24,0},{28,4},{1,9},{5... | collective-permute-start | bytes 1376264 | tf_op jit(solution)/shard_map/ppermute | solution.py:144
  53.2 12.7 %collective-permute-start.5 = (bf16[128,3584]{1,0:T(8,128)(2,1)S(1)}, bf16[128,3584]{1,0:T(8,128)(2,1)S(1)}, u32[]{:S(2)}, u32[]{:S(2)}) collective-permute-start(bf16[128,3584]{1,0:T(8,128)(2,1)S(1)} %collective-permute-done.4), channel_id=1, source_target_pairs={{0,1},{1,0},{2,3},{3,2},{4,5},{5,4},{6,7},{7,6},{8,9},{9,8},{10,11... | collective-permute-start | bytes 2752520 | tf_op jit(solution)/shard_map/ppermute | solution.py:123
  63.2 10.9 %collective-permute-start.12 = (bf16[448,512]{1,0:T(8,128)(2,1)S(1)}, bf16[448,512]{1,0:T(8,128)(2,1)S(1)}, u32[]{:S(2)}, u32[]{:S(2)}) collective-permute-start(bf16[448,512]{1,0:T(8,128)(2,1)S(1)} %collective-permute-done.11), channel_id=1, source_target_pairs={{0,4},{4,0},{8,12},{12,8},{16,20},{20,16},{24,28},{28,24},{1,5},{5... | collective-permute-start | bytes 1376264 | tf_op jit(solution)/shard_map/ppermute | solution.py:123
  75.0 12.7 %copy-start.16 = (s32[1,128]{1,0:T(1,128)S(1)}, s32[1,128]{1,0:T(1,128)}, u32[]{:S(2)}) copy-start(s32[1,128]{1,0:T(1,128)} %param.10) | copy-start | bytes 1540
  75.0 14.2 %copy-start = (bf16[1,128,3584]{2,1,0:T(8,128)(2,1)S(1)}, bf16[1,128,3584]{2,1,0:T(8,128)(2,1)}, u32[]{:S(2)}) copy-start(bf16[1,128,3584]{2,1,0:T(8,128)(2,1)} %param.7) | copy-start | bytes 2752516
  75.0 14.2 %copy-start.1 = (bf16[1,128,3584]{2,1,0:T(8,128)(2,1)S(1)}, bf16[1,128,3584]{2,1,0:T(8,128)(2,1)}, u32[]{:S(2)}) copy-start(bf16[1,128,3584]{2,1,0:T(8,128)(2,1)} %param.8) | copy-start | bytes 2752516
  80.5 6.4 %collective-permute-start.14 = (bf16[512,256]{1,0:T(8,128)(2,1)S(1)}, bf16[512,256]{1,0:T(8,128)(2,1)S(1)}, u32[]{:S(2)}, u32[]{:S(2)}) collective-permute-start(bf16[512,256]{1,0:T(8,128)(2,1)S(1)} %fusion.17.refs_0_), channel_id=1, source_target_pairs={{0,2},{1,3},{2,0},{3,1},{4,6},{5,7},{6,4},{7,5},{8,10},{9,11},{10,... | collective-permute-start | bytes 786440 | tf_op jit(solution)/shard_map/ppermute | solution.py:123
  86.9 1.5 collective-permute-start.15
  87.8 16.2 %collective-permute-start.13 = (bf16[512,256]{1,0:T(8,128)(2,1)S(1)}, bf16[512,256]{1,0:T(8,128)(2,1)}, u32[]{:S(2)}, u32[]{:S(2)}) collective-permute-start(bf16[512,256]{1,0:T(8,128)(2,1)S(1)} %fusion.17.refs_0_), channel_id=1, source_target_pairs={{0,1},{1,0},{2,3},{3,2},{4,5},{5,4},{6,7},{7,6},{8,9},{9,8},{10,11... | collective-permute-start | bytes 786440 | tf_op jit(solution)/shard_map/ppermute | solution.py:123
  89.2 1.0 copy-start.4
  103.3 15.5 %collective-permute-start.17 = (f32[512,256]{1,0:T(8,128)}, f32[512,256]{1,0:T(8,128)}, u32[]{:S(2)}, u32[]{:S(2)}) collective-permute-start(f32[512,256]{1,0:T(8,128)} %slice_bitcast_fusion), channel_id=1, source_target_pairs={{0,1},{1,0},{2,3},{3,2},{4,5},{5,4},{6,7},{7,6},{8,9},{9,8},{10,11... | collective-permute-start | bytes 1572872 | tf_op jit(solution)/shard_map/ppermute | solution.py:123
  103.4 26.3 %collective-permute-start.30 = (bf16[8,128,512]{1,2,0:T(8,128)(2,1)}, bf16[8,128,512]{1,2,0:T(8,128)(2,1)}, u32[]{:S(2)}, u32[]{:S(2)}) collective-permute-start(bf16[8,128,512]{1,2,0:T(8,128)(2,1)} %all-to-all-done), channel_id=1, source_target_pairs={{0,2},{1,3},{2,0},{3,1},{4,6},{5,7},{6,4},{7,5},{8,10},{9,11},{10,... | collective-permute-start | bytes 3145736 | tf_op jit(solution)/shard_map/ppermute | solution.py:123
  104.0 28.1 %collective-permute-start.29 = (bf16[8,128,512]{1,2,0:T(8,128)(2,1)}, bf16[8,128,512]{1,2,0:T(8,128)(2,1)}, u32[]{:S(2)}, u32[]{:S(2)}) collective-permute-start(bf16[8,128,512]{1,2,0:T(8,128)(2,1)} %all-to-all-done), channel_id=1, source_target_pairs={{0,1},{1,0},{2,3},{3,2},{4,5},{5,4},{6,7},{7,6},{8,9},{9,8},{10,11... | collective-permute-start | bytes 3145736 | tf_op jit(solution)/shard_map/ppermute | solution.py:123
  104.0 1.2 copy-start.2
  118.4 16.0 %collective-permute-start.16 = (f32[512,256]{1,0:T(8,128)}, f32[512,256]{1,0:T(8,128)}, u32[]{:S(2)}, u32[]{:S(2)}) collective-permute-start(f32[512,256]{1,0:T(8,128)} %slice_bitcast_fusion.1), channel_id=1, source_target_pairs={{0,1},{1,0},{2,3},{3,2},{4,5},{5,4},{6,7},{7,6},{8,9},{9,8},{10,11... | collective-permute-start | bytes 1572872 | tf_op jit(solution)/shard_map/ppermute | solution.py:123
  120.7 19.7 %collective-permute-start.18 = (f32[512,256]{1,0:T(8,128)}, f32[512,256]{1,0:T(8,128)}, u32[]{:S(2)}, u32[]{:S(2)}) collective-permute-start(f32[512,256]{1,0:T(8,128)} %bitcast_add_fusion), channel_id=1, source_target_pairs={{0,2},{1,3},{2,0},{3,1},{4,6},{5,7},{6,4},{7,5},{8,10},{9,11},{10,... | collective-permute-start | bytes 1572872 | tf_op jit(solution)/shard_map/ppermute | solution.py:123
  122.8 61.5 %collective-permute-start.20 = (bf16[3584,512]{1,0:T(8,128)(2,1)}, bf16[3584,512]{1,0:T(8,128)(2,1)}, u32[]{:S(2)}, u32[]{:S(2)}) collective-permute-start(bf16[3584,512]{1,0:T(8,128)(2,1)} %bitcast.26), channel_id=1, source_target_pairs={{0,1},{1,0},{2,3},{3,2},{4,5},{5,4},{6,7},{7,6},{8,9},{9,8},{10,11... | collective-permute-start | bytes 11010056 | tf_op jit(solution)/shard_map/ppermute | solution.py:123
  124.3 10.1 %copy-start.10 = (bf16[8,128,512]{2,1,0:T(8,128)(2,1)}, bf16[8,128,512]{2,1,0:T(8,128)(2,1)S(1)}, u32[]{:S(2)}) copy-start(bf16[8,128,512]{2,1,0:T(8,128)(2,1)S(1)} %copy.25) | copy-start | bytes 3145732
  129.7 34.5 %collective-permute-start.31 = (bf16[8,128,512]{1,2,0:T(8,128)(2,1)}, bf16[8,128,512]{1,2,0:T(8,128)(2,1)}, u32[]{:S(2)}, u32[]{:S(2)}) collective-permute-start(bf16[8,128,512]{1,2,0:T(8,128)(2,1)} %collective-permute-done.30), channel_id=1, source_target_pairs={{0,1},{1,0},{2,3},{3,2},{4,5},{5,4},{6,7},{7,6},{8,9},{9,8},{10,11... | collective-permute-start | bytes 3145736 | tf_op jit(solution)/shard_map/ppermute | solution.py:123
  141.8 12.4 %collective-permute-start.22 = (bf16[512,256]{1,0:T(8,128)(2,1)S(1)}, bf16[512,256]{1,0:T(8,128)(2,1)S(1)}, u32[]{:S(2)}, u32[]{:S(2)}) collective-permute-start(bf16[512,256]{1,0:T(8,128)(2,1)S(1)} %get-tuple-element.25), channel_id=1, source_target_pairs={{0,4},{4,0},{8,12},{12,8},{16,20},{20,16},{24,28},{28,24},{1,5},{5... | collective-permute-start | bytes 786440 | tf_op jit(solution)/shard_map/ppermute | solution.py:123
  143.3 10.3 %collective-permute-start.23 = (bf16[512,256]{1,0:T(8,128)(2,1)S(1)}, bf16[512,256]{1,0:T(8,128)(2,1)}, u32[]{:S(2)}, u32[]{:S(2)}) collective-permute-start(bf16[512,256]{1,0:T(8,128)(2,1)S(1)} %get-tuple-element.25), channel_id=1, source_target_pairs={{0,8},{4,12},{8,16},{12,20},{16,24},{20,28},{24,0},{28,4},{1,9},{5... | collective-permute-start | bytes 786440 | tf_op jit(solution)/shard_map/ppermute | solution.py:144
  149.1 6.2 %collective-permute-start.19 = (bf16[512,256]{1,0:T(8,128)(2,1)S(1)}, bf16[512,256]{1,0:T(8,128)(2,1)S(1)}, u32[]{:S(2)}, u32[]{:S(2)}) collective-permute-start(bf16[512,256]{1,0:T(8,128)(2,1)S(1)} %get-tuple-element.25), channel_id=1, source_target_pairs={{0,1},{1,0},{2,3},{3,2},{4,5},{5,4},{6,7},{7,6},{8,9},{9,8},{10,11... | collective-permute-start | bytes 786440 | tf_op jit(solution)/shard_map/ppermute | solution.py:123
  153.6 12.2 %collective-permute-start.24 = (bf16[512,256]{1,0:T(8,128)(2,1)}, bf16[512,256]{1,0:T(8,128)(2,1)}, u32[]{:S(2)}, u32[]{:S(2)}) collective-permute-start(bf16[512,256]{1,0:T(8,128)(2,1)} %collective-permute-done.23), channel_id=1, source_target_pairs={{0,4},{4,0},{8,12},{12,8},{16,20},{20,16},{24,28},{28,24},{1,5},{5... | collective-permute-start | bytes 786440 | tf_op jit(solution)/shard_map/ppermute | solution.py:123
  154.2 8.7 %collective-permute-start.25 = (bf16[512,256]{1,0:T(8,128)(2,1)}, bf16[512,256]{1,0:T(8,128)(2,1)}, u32[]{:S(2)}, u32[]{:S(2)}) collective-permute-start(bf16[512,256]{1,0:T(8,128)(2,1)} %collective-permute-done.23), channel_id=1, source_target_pairs={{0,8},{4,12},{8,16},{12,20},{16,24},{20,28},{24,0},{28,4},{1,9},{5... | collective-permute-start | bytes 786440 | tf_op jit(solution)/shard_map/ppermute | solution.py:144
  162.9 10.5 %collective-permute-start.26 = (bf16[512,256]{1,0:T(8,128)(2,1)}, bf16[512,256]{1,0:T(8,128)(2,1)}, u32[]{:S(2)}, u32[]{:S(2)}) collective-permute-start(bf16[512,256]{1,0:T(8,128)(2,1)} %collective-permute-done.25), channel_id=1, source_target_pairs={{0,4},{4,0},{8,12},{12,8},{16,20},{20,16},{24,28},{28,24},{1,5},{5... | collective-permute-start | bytes 786440 | tf_op jit(solution)/shard_map/ppermute | solution.py:123
  164.3 8.5 %collective-permute-start.27 = (bf16[512,256]{1,0:T(8,128)(2,1)}, bf16[512,256]{1,0:T(8,128)(2,1)}, u32[]{:S(2)}, u32[]{:S(2)}) collective-permute-start(bf16[512,256]{1,0:T(8,128)(2,1)} %collective-permute-done.25), channel_id=1, source_target_pairs={{0,8},{4,12},{8,16},{12,20},{16,24},{20,28},{24,0},{28,4},{1,9},{5... | collective-permute-start | bytes 786440 | tf_op jit(solution)/shard_map/ppermute | solution.py:144
  168.2 11.8 %copy-start.14 = (pred[1024]{0:T(1024)(128)(4,1)S(1)}, pred[1024]{0:T(1024)(128)(4,1)}, u32[]{:S(2)}) copy-start(pred[1024]{0:T(1024)(128)(4,1)} %get-tuple-element.18) | copy-start | bytes 3076
  168.2 11.8 %copy-start.15 = (pred[1024]{0:T(1024)(128)(4,1)S(1)}, pred[1024]{0:T(1024)(128)(4,1)}, u32[]{:S(2)}) copy-start(pred[1024]{0:T(1024)(128)(4,1)} %get-tuple-element.19) | copy-start | bytes 3076
  172.8 6.6 %collective-permute-start.28 = (bf16[512,256]{1,0:T(8,128)(2,1)}, bf16[512,256]{1,0:T(8,128)(2,1)S(1)}, u32[]{:S(2)}, u32[]{:S(2)}) collective-permute-start(bf16[512,256]{1,0:T(8,128)(2,1)} %collective-permute-done.27), channel_id=1, source_target_pairs={{0,4},{4,0},{8,12},{12,8},{16,20},{20,16},{24,28},{28,24},{1,5},{5... | collective-permute-start | bytes 786440 | tf_op jit(solution)/shard_map/ppermute | solution.py:123
  179.4 1.2 copy-start.11
  180.6 1.7 copy-start.9
  182.3 1.2 copy-start.8
  183.1 1.2 copy-start.12
  183.1 1.2 copy-start.13
  191.0 17.2 %collective-permute-start.21 = (bf16[128,3584]{1,0:T(8,128)(2,1)S(1)}, bf16[128,3584]{1,0:T(8,128)(2,1)S(1)}, u32[]{:S(2)}, u32[]{:S(2)}) collective-permute-start(bf16[128,3584]{1,0:T(8,128)(2,1)S(1)} %fusion.2), channel_id=1, source_target_pairs={{0,2},{1,3},{2,0},{3,1},{4,6},{5,7},{6,4},{7,5},{8,10},{9,11},{10,... | collective-permute-start | bytes 2752520 | tf_op jit(solution)/shard_map/ppermute | solution.py:123
  (3 other events, 2.4 us)
where the time goes:
time: 214 us; the launch traced here: 212 us
  waiting for transfers between devices  79.8 us (37%)
  local copies, waits for them, and re-layouts  39.8 us (19%)
  starting transfers between devices  29.9 us (14%)
  Pallas kernels  23.7 us (11%)
  matrix products  22.6 us (11%)
  other arithmetic  15.7 us (7%)
    ppermute x26, waiting for transfers between devices, swap(): return lax.ppermute(x, axis, [(i, i ^ bit) for i in range(size)])  48 us
    ppermute x6, waiting for transfers between devices, over_fsdp(): x = lax.ppermute(x, 'fsdp', [(i, (i + 2) % fsdp) for i in range(fsdp)])  31.8 us
    pallas_call x2, Pallas kernels, attend(): pl.pallas_call(functools.partial(attend_kernel, count), grid_spec=pltpu.P...  23.7 us
    dot_general x8, matrix products, contract(): lax.dot_general(a, b, (((da,), (db,)), ((), ())), preferred_element_type=...  17.2 us
    ppermute x26, starting transfers between devices, swap(): return lax.ppermute(x, axis, [(i, i ^ bit) for i in range(size)])  16.6 us
    ppermute x6, starting transfers between devices, over_fsdp(): x = lax.ppermute(x, 'fsdp', [(i, (i + 2) % fsdp) for i in range(fsdp)])  8.98 us
    unnamed x37, local copies, waits for them, and re-layouts  6.77 us
    dynamic_update_slice x6, local copies, waits for them, and re-layouts, over_fsdp(): whole = lax.dynamic_update_index_in_dim(whole, x, owner, 0)  6.4 us
  transfers between devices with their start and end apart: 33, of which 14 were waited for; matrix products, arithmetic and copies ran while one was open for 28% of the time, Pallas kernels for 11%

commit v1 on v0

v1 whole, which is shorter than its diff:
```python
import functools

import jax
import jax.numpy as jnp
from jax import lax
from jax.experimental import pallas as pl
from jax.experimental.pallas import tpu as pltpu
from jax.sharding import PartitionSpec as P

HEAD_DIM = 128
GROUP = 7
SCALE = HEAD_DIM ** (-0.5)
LOG2E = 1.4426950408889634
HIDDEN = -1e30
F32 = jnp.float32
BF16 = jnp.bfloat16


def contract(a, b, da, db):
    return lax.dot_general(a, b, (((da,), (db,)), ((), ())), preferred_element_type=F32)


def after(x, *others):
    return pl.pallas_call(
        lambda *refs: None,
        in_specs=[pl.BlockSpec(memory_space=pl.ANY)] * (1 + len(others)),
        out_specs=pl.BlockSpec(memory_space=pl.ANY),
        out_shape=jax.ShapeDtypeStruct(x.shape, x.dtype),
        input_output_aliases={0: 0},
        cost_estimate=pl.CostEstimate(flops=0, bytes_accessed=0, transcendentals=0),
    )(x, *others)


def attend_kernel(count, heads_ref, q_ref, up_ref, *refs):
    kv_refs, (qb_ref, kb_ref) = refs[:count], refs[count : count + 2]
    att_ref, gq_ref, gkv_ref, bias, scores_all, dp_all, pbs, his, los = refs[-9:]
    rows = q_ref.shape[0]
    step = pl.program_id(0)

    @pl.when(step == 0)
    def _():
        bias[...] = jnp.where(kb_ref[...] <= qb_ref[...], 0.0, HIDDEN).astype(F32)

    kv = kv_refs[0][...]
    for r in range(1, count):
        kv = jnp.where(step == r, kv_refs[r][...], kv)
    keys = kv[:, :HEAD_DIM]
    values = kv[:, HEAD_DIM:]
    heads = [slice(h * HEAD_DIM, (h + 1) * HEAD_DIM) for h in range(GROUP)]
    q = jnp.concatenate([q_ref[:, cols] for cols in heads], axis=0)
    up = jnp.concatenate([up_ref[:, cols] for cols in heads], axis=0)
    scores_all[...] = contract(q, keys, 1, 1)
    dp_all[...] = contract(up, values, 1, 1).astype(BF16)
    for h in range(GROUP):
        here = slice(h * rows, (h + 1) * rows)
        scores = scores_all[here, :] * (SCALE * LOG2E) + bias[...]
        expo = jnp.exp2(scores - jnp.max(scores, axis=-1, keepdims=True))
        probs = expo * (1.0 / jnp.sum(expo, axis=-1, keepdims=True))
        pbs[here, :] = probs.astype(BF16)
        dp = dp_all[here, :].astype(F32)
        ds = probs * (dp - jnp.sum(probs * dp, axis=-1, keepdims=True))
        hi = ds.astype(BF16)
        his[here, :] = hi
        los[here, :] = (ds - hi.astype(F32)).astype(BF16)
    att = contract(pbs[...], values, 1, 0).astype(BF16)
    gq = ((contract(his[...], keys, 1, 0) + contract(los[...], keys, 1, 0)) * SCALE).astype(BF16)
    for h, cols in enumerate(heads):
        att_ref[:, cols] = att[h * rows : (h + 1) * rows, :]
        gq_ref[:, cols] = gq[h * rows : (h + 1) * rows, :]
    dk = (contract(q, his[...], 0, 0) + contract(q, los[...], 0, 0)) * SCALE
    dv = contract(up, pbs[...], 0, 0)
    gkv_ref[0, :, :HEAD_DIM] = dk.T
    gkv_ref[0, :, HEAD_DIM:] = dv.T


def attend(heads, queries, upstream, kvs, query_blocks, key_blocks, before=(), wait=()):
    rows, width = queries.shape
    length, pair = kvs[0].shape
    count = len(kvs)
    span = GROUP * HEAD_DIM
    by_head = pl.BlockSpec((rows, span), lambda r, heads: (0, heads[r]))
    whole = pl.BlockSpec((length, pair), lambda r, heads: (0, 0))
    stacked = (GROUP * rows, length)
    return pl.pallas_call(
        functools.partial(attend_kernel, count),
        grid_spec=pltpu.PrefetchScalarGridSpec(
            num_scalar_prefetch=1,
            grid=(count,),
            in_specs=[by_head, by_head]
            + [whole] * count
            + [
                pl.BlockSpec((rows, 1), lambda r, heads: (0, 0)),
                pl.BlockSpec((1, length), lambda r, heads: (0, 0)),
            ]
            + [pl.BlockSpec(memory_space=pl.ANY)] * (len(before) + len(wait)),
            out_specs=[
                by_head,
                by_head,
                pl.BlockSpec((1, length, pair), lambda r, heads: (r, 0, 0)),
            ],
            scratch_shapes=[
                pltpu.VMEM((rows, length), F32),
                pltpu.VMEM(stacked, F32),
                pltpu.VMEM(stacked, BF16),
                pltpu.VMEM(stacked, BF16),
                pltpu.VMEM(stacked, BF16),
                pltpu.VMEM(stacked, BF16),
            ],
        ),
        out_shape=[
            jax.ShapeDtypeStruct((rows, width), BF16),
            jax.ShapeDtypeStruct((rows, width), BF16),
            jax.ShapeDtypeStruct((count, length, pair), F32),
        ],
        input_output_aliases={5 + count + i: i for i in range(len(before))},
        compiler_params=pltpu.CompilerParams(vmem_limit_bytes=32 * 1024 * 1024),
        cost_estimate=pl.CostEstimate(
            flops=2 * 7 * count * GROUP * rows * length * HEAD_DIM,
            bytes_accessed=8 * rows * count * span + 6 * count * length * pair,
            transcendentals=count * GROUP * rows * length,
        ),
    )(heads, queries, upstream, *kvs, query_blocks, key_blocks, *before, *wait)


def by_expert(kind, x):
    zero = jnp.zeros_like(x)
    return jnp.concatenate([jnp.where(kind == e, x, zero) for e in range(2)], axis=-1)


def hidden_kernel(quarters_ref, kind_ref, g_ref, gc_ref, w_ref, wc_ref, mine_ref, away_ref):
    rows = mine_ref.shape[0]
    sides = []
    for i in range(2):
        here = pl.ds(pl.multiple_of(quarters_ref[i] * rows, rows), rows)
        kind = kind_ref[here, :]
        sides.append([by_expert(kind, ref[here, :].astype(F32)).astype(BF16) for ref in (g_ref, gc_ref)])
    g = jnp.concatenate([sides[0][0], sides[1][0]], axis=0)
    gc = jnp.concatenate([sides[0][1], sides[1][1]], axis=0)
    total = contract(g, w_ref[...], 1, 1) + contract(gc, wc_ref[...], 1, 1)
    mine_ref[...] = total[:rows]
    away_ref[...] = total[rows:].astype(BF16)


def hidden_grad(quarters, kind, grad, grad_c, weight, weight_c, rows):
    width, span = weight.shape
    length, pair = grad.shape
    tile = 512
    whole = pl.BlockSpec((length, pair), lambda i, q: (0, 0))
    by_tile = pl.BlockSpec((tile, span), lambda i, q: (i, 0))
    out = pl.BlockSpec((rows, tile), lambda i, q: (0, i))
    return pl.pallas_call(
        hidden_kernel,
        grid_spec=pltpu.PrefetchScalarGridSpec(
            num_scalar_prefetch=1,
            grid=(width // tile,),
            in_specs=[pl.BlockSpec((length, 1), lambda i, q: (0, 0)), whole, whole, by_tile, by_tile],
            out_specs=[out, out],
        ),
        out_shape=[jax.ShapeDtypeStruct((rows, width), F32), jax.ShapeDtypeStruct((rows, width), BF16)],
        compiler_params=pltpu.CompilerParams(vmem_limit_bytes=24 * 1024 * 1024),
        cost_estimate=pl.CostEstimate(
            flops=8 * rows * width * span, bytes_accessed=4 * width * span + 6 * rows * width, transcendentals=0
        ),
    )(quarters, kind, grad, grad_c, weight, weight_c)


def weight_kernel(depth, quarters_ref, *refs):
    part_refs, (g_ref, out_ref, total) = refs[:-3], refs[-3:]
    step = pl.program_id(0)
    seqs, rows, lanes = part_refs[0].shape
    pair = g_ref.shape[-1]
    part = part_refs[0][...]
    for r in range(1, len(part_refs)):
        part = jnp.where(step == r, part_refs[r][...], part)
    part = part.reshape(seqs * rows, lanes)
    kind = part[:, depth : depth + 1].astype(F32)
    grads = g_ref[...].reshape(seqs * rows, pair).astype(F32)
    product = contract(part, by_expert(kind, grads).astype(BF16), 0, 0)

    @pl.when(step == 0)
    def _():
        total[...] = product

    @pl.when(step != 0)
    def _():
        total[...] += product

    @pl.when(step == len(part_refs) - 1)
    def _():
        for e in range(2):
            out_ref[e] = total[:depth, e * pair : (e + 1) * pair]


def weight_grad(quarters, parts, grads, depth):
    seqs, rows, lanes = parts[0].shape
    pair = grads.shape[-1]
    count = len(parts)
    return pl.pallas_call(
        functools.partial(weight_kernel, depth),
        grid_spec=pltpu.PrefetchScalarGridSpec(
            num_scalar_prefetch=1,
            grid=(count,),
            in_specs=[pl.BlockSpec((seqs, rows, lanes), lambda r, q: (0, 0, 0))] * count
            + [pl.BlockSpec((seqs, rows, pair), lambda r, q: (0, q[r], 0))],
            out_specs=pl.BlockSpec((2, depth, pair), lambda r, q: (0, 0, 0)),
            scratch_shapes=[pltpu.VMEM((lanes, 2 * pair), F32)],
        ),
        out_shape=jax.ShapeDtypeStruct((2, depth, pair), F32),
        compiler_params=pltpu.CompilerParams(vmem_limit_bytes=40 * 1024 * 1024),
        cost_estimate=pl.CostEstimate(
            flops=4 * count * seqs * rows * lanes * pair,
            bytes_accessed=2 * count * seqs * rows * (lanes + pair) + 8 * depth * pair,
            transcendentals=0,
        ),
    )(quarters, *parts, grads)


def per_device(fsdp, seq, tokens, queries, cotangent, modality, block_ids, kv_weight):
    tokens, queries, cotangent = tokens[0], queries[0], cotangent[0]
    me_f = lax.axis_index("fsdp")
    me_s = lax.axis_index("seq")
    rows, width = tokens.shape
    depth, pair = kv_weight.shape[1:]
    length = seq * rows

    def swap(x, bit):
        return lax.ppermute(x, "seq", [(i, i ^ bit) for i in range(seq)])

    def over_seq(x):
        across = swap(x, 2)
        return [x, swap(x, 1), across, swap(across, 1)]

    def place(parts):
        whole = jnp.zeros((seq, *parts[0].shape), parts[0].dtype)
        for r, part in enumerate(parts):
            whole = lax.dynamic_update_index_in_dim(whole, part, me_s ^ r, 0)
        return whole

    def over_fsdp(x, hold=None):
        if fsdp != 8:
            return lax.all_gather(x, "fsdp", axis=0)
        cycle = [0, 2, 4, 6, 7, 5, 3, 1]
        order = jnp.array(cycle, jnp.int32)
        spot = jnp.array([cycle.index(i) for i in range(fsdp)], jnp.int32)[me_f]

        def turn(y, by):
            return lax.ppermute(y, "fsdp", [(cycle[i], cycle[(i + by) % fsdp]) for i in range(fsdp)])

        whole = jnp.zeros((fsdp, *x.shape), x.dtype)
        whole = lax.dynamic_update_index_in_dim(whole, x, me_f, 0)
        half = x.shape[0] // 2
        ups, downs = x, x
        for step in range(1, 5):
            if step == 2 and hold is not None:
                ups, downs = after(ups, *hold), after(downs, *hold)
            if step == 4:
                ups, downs = ups[:half], downs[half:]
            ups, downs = turn(ups, 1), turn(downs, -1)
            before = order[lax.rem(spot + fsdp - step, fsdp)]
            behind = order[lax.rem(spot + step, fsdp)]
            whole = lax.dynamic_update_slice(whole, ups[None], (before, 0, 0))
            whole = lax.dynamic_update_slice(whole, downs[None], (behind, half if step == 4 else 0, 0))
        return whole

    both = jnp.concatenate([kv_weight[0], kv_weight[1]], axis=-1)
    weight = over_fsdp(both).reshape(width, 2 * pair)
    hidden = place(over_seq(tokens)).reshape(length, width)
    ids = place(over_seq(jnp.stack([modality[0], block_ids[0]])))
    modal_here = ids[:, 0].reshape(length, 1)
    blocks_here = ids[:, 1].reshape(1, length)

    parts = jnp.dot(hidden, weight, preferred_element_type=F32)
    key_value = jnp.where(modal_here == 1, parts[:, pair:], parts[:, :pair]).astype(BF16)

    kvs = over_seq(key_value)
    heads = me_s ^ jnp.arange(seq, dtype=jnp.int32)
    given = (block_ids[0][:, None], blocks_here)
    out_a, out_q, far_c = attend(heads[3:], queries, cotangent, kvs[3:], *given)
    out_a, out_q, far = attend(heads[2:3], queries, cotangent, kvs[2:3], *given, (out_a, out_q))
    far = far[0] + swap(far_c[0], 1)
    attended, grad_queries, near = attend(heads[:2], queries, cotangent, kvs[:2], *given, (out_a, out_q), (far,))
    grad_kv = (near[0] + swap(near[1], 1) + swap(far, 2)).astype(BF16)

    lanes = -(-(depth + 1) // 128) * 128
    columns = tokens.reshape(rows, fsdp, depth).transpose(1, 0, 2)
    kinds = jnp.broadcast_to(modality[0].astype(BF16)[None, :, None], (fsdp, rows, 1))
    blank = jnp.zeros((fsdp, rows, lanes - depth - 1), BF16)
    columns = jnp.concatenate([columns, kinds, blank], axis=-1)
    columns = lax.all_to_all(columns, "fsdp", split_axis=0, concat_axis=0, tiled=True)
    columns = over_seq(columns)

    weight_c = swap(weight, 1)
    mine, away = hidden_grad(
        jnp.stack([me_s, me_s ^ 2]), modal_here, grad_kv, swap(grad_kv, 1), weight, weight_c, rows
    )
    grad_weight = weight_grad(heads, columns, over_fsdp(grad_kv, (away,)), depth)
    grad_tokens = (mine + swap(away, 2).astype(F32)).astype(BF16)
    return attended[None], grad_queries[None], grad_tokens[None], grad_weight


def solution(mesh):
    split = P("fsdp", "seq", None)
    weights = P(None, "fsdp", "seq")
    return jax.shard_map(
        functools.partial(per_device, mesh.shape["fsdp"], mesh.shape["seq"]),
        mesh=mesh,
        in_specs=(split, split, split, P("fsdp", "seq"), P("fsdp", "seq"), weights),
        out_specs=(split, split, split, weights),
        check_vma=False,
    )
```

time: 214 us -> 177 us (0.83)
  waiting for transfers between devices: 79.8 us -> 56.1 us
  between operations: 1.02 us -> 19.1 us
  matrix products: 22.6 us -> 5.33 us
  local copies, waits for them, and re-layouts: 39.8 us -> 27.3 us
  other arithmetic: 15.7 us -> 6.32 us
  Pallas kernels: 23.7 us -> 28.1 us
  starting transfers between devices: 29.9 us -> 34.1 us
    ppermute x32 -> x34, waiting for transfers between devices: 79.8 us -> 50 us  [the longest x16 30.9 us: turn(): lax.ppermute(y, 'fsdp', [(cycle[i], cycle[(i + by) % fsdp]) for i in rang...]
    dot_general x8 -> x0, matrix products: 17.2 us -> none  [contract(): lax.dot_general(a, b, (((da,), (db,)), ((), ())), preferred_element_type=...]
    pallas_call x0 -> x4, Pallas kernels: none -> 15.4 us  [the longest x1 8.01 us: weight_grad(): pl.pallas_call(functools.partial(weight_kernel, depth), grid_spec=pltpu.P...]
    pallas_call x2 -> x3, Pallas kernels: 23.7 us -> 12.7 us  [attend(): pl.pallas_call(functools.partial(attend_kernel, count), grid_spec=pltpu.P...]
    all_to_all x1, waiting for transfers between devices: 0.01 us -> 6.15 us  [per_device(): lax.all_to_all(columns, 'fsdp', split_axis=0, concat_axis=0, tiled=True)]
    ppermute x3 -> x0, local copies, waits for them, and re-layouts: 6.07 us -> none  [swap(): return lax.ppermute(x, axis, [(i, i ^ bit) for i in range(size)])]
    eq x4 -> x0, other arithmetic: 4.2 us -> none  [by_expert(): kind == e]
    dynamic_update_slice x14 -> x16, local copies, waits for them, and re-layouts: 12.6 us -> 8.5 us  [the longest x8 4.26 us: over_fsdp(): whole = lax.dynamic_update_slice(whole, ups[None], (before, 0, 0))]
  transfers between devices with their start and end apart: 33 -> 35, of which waited for: 14 -> 13; matrix products, arithmetic and copies ran while one was open for 28% -> 20% of each run, Pallas kernels for 11% -> 16%
where the time goes in v1:
time: 177 us; the launch traced here: 176 us
  waiting for transfers between devices  56.1 us (32%)
  starting transfers between devices  34.1 us (19%)
  Pallas kernels  28.1 us (16%)
  local copies, waits for them, and re-layouts  27.3 us (15%)
  between operations  19.1 us (11%)
  other arithmetic  6.32 us (4%)
  matrix products  5.33 us (3%)
    ppermute x16, waiting for transfers between devices, turn(): lax.ppermute(y, 'fsdp', [(cycle[i], cycle[(i + by) % fsdp]) for i in rang...  30.9 us
    ppermute x18, waiting for transfers between devices, swap(): return lax.ppermute(x, 'seq', [(i, i ^ bit) for i in range(seq)])  19.1 us
    ppermute x16, starting transfers between devices, turn(): lax.ppermute(y, 'fsdp', [(cycle[i], cycle[(i + by) % fsdp]) for i in rang...  18.8 us
    pallas_call x3, Pallas kernels, attend(): pl.pallas_call(functools.partial(attend_kernel, count), grid_spec=pltpu.P...  12.7 us
    ppermute x18, starting transfers between devices, swap(): return lax.ppermute(x, 'seq', [(i, i ^ bit) for i in range(seq)])  10.2 us
    pallas_call x1, Pallas kernels, weight_grad(): pl.pallas_call(functools.partial(weight_kernel, depth), grid_spec=pltpu.P...  8.01 us
    pallas_call x1, Pallas kernels, hidden_grad(): pl.pallas_call(hidden_kernel, grid_spec=pltpu.PrefetchScalarGridSpec(num_...  7.43 us
    all_to_all x1, waiting for transfers between devices, per_device(): lax.all_to_all(columns, 'fsdp', split_axis=0, concat_axis=0, tiled=True)  6.15 us
  transfers between devices with their start and end apart: 35, of which 13 were waited for; matrix products, arithmetic and copies ran while one was open for 20% of the time, Pallas kernels for 16%

profile of v1, /device:TPU:0, one launch (start us, length us, event | category | flops | bytes accessed | tf_op | source)
XLA Modules:
  0.0 176.4 jit_solution(13444135076625284580)
XLA Ops:
  1.2 2.6 %collective-permute-start.4 = (bf16[128,3584]{1,0:T(8,128)(2,1)}, bf16[128,3584]{1,0:T(8,128)(2,1)S(1)}, u32[]{:S(2)}, u32[]{:S(2)}) collective-permute-start(bf16[128,3584]{1,0:T(8,128)(2,1)} %bitcast.120), channel_id=1, source_target_pairs={{0,2},{1,3},{2,0},{3,1},{4,6},{5,7},{6,4},{7,5},{8,10},{9,11},{10,... | collective-permute-start | bytes 2752520 | tf_op jit(solution)/shard_map/ppermute | solution.py:227
  3.8 1.1 slice_bitcast_fusion.2
  5.7 1.6 collective-permute-start.6
  8.4 2.1 %broadcast_in_dim.124 = bf16[4,128,3584]{2,1,0:T(8,128)(2,1)} broadcast(bf16[]{:T(256)} %constant.120.clone.1), dimensions={} | broadcast | bytes 3670018 | tf_op jit(solution)/shard_map/broadcast_in_dim | solution.py:234
  10.4 1.0 constant_dynamic-update-slice_fusion
  16.6 2.2 %broadcast_in_dim.128 = bf16[8,448,512]{2,1,0:T(8,128)(2,1)} broadcast(bf16[]{:T(256)} %constant.120.clone.1), dimensions={} | broadcast | bytes 3670018 | tf_op jit(solution)/shard_map/broadcast_in_dim | solution.py:249
  18.9 0.8 bitcast_dynamic-update-slice_fusion.9
  34.8 1.8 %collective-permute-start.8 = (bf16[448,512]{1,0:T(8,128)(2,1)}, bf16[448,512]{1,0:T(8,128)(2,1)S(1)}, u32[]{:S(2)}, u32[]{:S(2)}) collective-permute-start(bf16[448,512]{1,0:T(8,128)(2,1)} %collective-permute-done.6), channel_id=1, source_target_pairs={{0,8},{8,16},{16,24},{24,28},{28,20},{20,12},{12,4},{4,0},{1,9},{9... | collective-permute-start | bytes 1376264 | tf_op jit(solution)/shard_map/ppermute | solution.py:247
  36.9 1.9 %bitcast_dynamic-update-slice_fusion.8 = bf16[8,448,512]{2,1,0:T(8,128)(2,1)} fusion(bf16[8,448,512]{2,1,0:T(8,128)(2,1)} %bitcast_dynamic-update-slice_fusion.9, s32[]{:T(128)S(6)} %select_n.124, bf16[448,512]{1,0:T(8,128)(2,1)} %collective-permute-done.6), kind=kLoop, calls=%fused_computation.19 | loop fusion | bytes 917508 | tf_op jit(solution)/shard_map/dynamic_update_slice | solution.py:261
  38.7 1.9 %bitcast_dynamic-update-slice_fusion.7 = bf16[8,448,512]{2,1,0:T(8,128)(2,1)} fusion(bf16[8,448,512]{2,1,0:T(8,128)(2,1)} %bitcast_dynamic-update-slice_fusion.8, s32[]{:T(128)S(6)} %select_n.126, bf16[448,512]{1,0:T(8,128)(2,1)} %collective-permute-done.7), kind=kLoop, calls=%fused_computation.18 | loop fusion | bytes 917508 | tf_op jit(solution)/shard_map/dynamic_update_slice | solution.py:262
  40.6 1.0 bitcast_dynamic-update-slice_fusion.2
  41.6 1.0 bitcast_dynamic-update-slice_fusion.1
  42.6 5.1 %collective-permute-done.8 = bf16[448,512]{1,0:T(8,128)(2,1)S(1)} collective-permute-done((bf16[448,512]{1,0:T(8,128)(2,1)}, bf16[448,512]{1,0:T(8,128)(2,1)S(1)}, u32[]{:S(2)}, u32[]{:S(2)}) %collective-permute-start.8) | collective-permute-done | bytes 458784 | tf_op jit(solution)/shard_map/ppermute | solution.py:247
  47.7 1.8 %collective-permute-start.10 = (bf16[448,512]{1,0:T(8,128)(2,1)S(1)}, bf16[448,512]{1,0:T(8,128)(2,1)S(1)}, u32[]{:S(2)}, u32[]{:S(2)}) collective-permute-start(bf16[448,512]{1,0:T(8,128)(2,1)S(1)} %collective-permute-done.8), channel_id=1, source_target_pairs={{0,8},{8,16},{16,24},{24,28},{28,20},{20,12},{12,4},{4,0},{1,9},{9... | collective-permute-start | bytes 1376264 | tf_op jit(solution)/shard_map/ppermute | solution.py:247
  51.3 8.3 %collective-permute-done.10 = bf16[448,512]{1,0:T(8,128)(2,1)S(1)} collective-permute-done((bf16[448,512]{1,0:T(8,128)(2,1)S(1)}, bf16[448,512]{1,0:T(8,128)(2,1)S(1)}, u32[]{:S(2)}, u32[]{:S(2)}) %collective-permute-start.10) | collective-permute-done | bytes 458784 | tf_op jit(solution)/shard_map/ppermute | solution.py:247
  59.7 1.9 %collective-permute-start.12 = (bf16[224,512]{1,0:T(8,128)(2,1)S(1)}, bf16[224,512]{1,0:T(8,128)(2,1)S(1)}, u32[]{:S(2)}, u32[]{:S(2)}) collective-permute-start(bf16[224,512]{1,0:T(8,128)(2,1)S(1)} %slice.61), channel_id=1, source_target_pairs={{0,8},{8,16},{16,24},{24,28},{28,20},{20,12},{12,4},{4,0},{1,9},{9... | collective-permute-start | bytes 688136 | tf_op jit(solution)/shard_map/ppermute | solution.py:247
  63.5 2.3 %collective-permute-done.12 = bf16[224,512]{1,0:T(8,128)(2,1)S(1)} collective-permute-done((bf16[224,512]{1,0:T(8,128)(2,1)S(1)}, bf16[224,512]{1,0:T(8,128)(2,1)S(1)}, u32[]{:S(2)}, u32[]{:S(2)}) %collective-permute-start.12) | collective-permute-done | bytes 229408 | tf_op jit(solution)/shard_map/ppermute | solution.py:247
  66.5 1.1 collective-permute-done.13
  68.4 1.0 bitcast_dynamic-update-slice_fusion
  69.4 5.3 %fusion.8 = bf16[512,512]{1,0:T(8,128)(2,1)S(1)} fusion(bf16[512,3584]{1,0:T(8,128)(2,1)} %bitcast.15, bf16[3584,512]{1,0:T(8,128)(2,1)} %bitcast.41.w_ref), kind=kOutput, calls=%fused_computation.43 | convolution fusion | flops 1879048192 | bytes 7864320 | tf_op jit(solution)/shard_map/dot_general | solution.py:272
  74.9 1.6 collective-permute-start.15
  76.4 7.2 %collective-permute-done.15.refs_0_ = bf16[512,256]{1,0:T(8,128)(2,1)S(1)} collective-permute-done((bf16[512,256]{1,0:T(8,128)(2,1)S(1)}, bf16[512,256]{1,0:T(8,128)(2,1)S(1)}, u32[]{:S(2)}, u32[]{:S(2)}) %collective-permute-start.15) | collective-permute-done | bytes 262176 | tf_op jit(solution)/shard_map/ppermute | solution.py:227
  85.2 3.5 %shard_map.129 = (bf16[128,3584]{1,0:T(8,128)(2,1)}, bf16[128,3584]{1,0:T(8,128)(2,1)}, f32[1,512,256]{2,1,0:T(8,128)S(1)}) custom-call(s32[1]{0:T(128)} %get-tuple-element.32.heads_ref, bf16[128,3584]{1,0:T(8,128)(2,1)S(1)} %bitcast.107, bf16[128,3584]{1,0:T(8,128)(2,1)S(1)} %bitcast.110, bf16[512,256]{1,0:T(8,128)(2,1)S(1)} %collective-permute-done.16.refs_0_, ...), custom_call_target="tpu_custom_call" | custom-call | flops 822083584 | bytes 1703936 | tf_op jit(solution)/shard_map/pallas_call | solution.py:84
  88.8 2.2 %copy.35 = bf16[1,128,3584]{1,2,0:T(8,128)(2,1)} copy(bf16[1,128,3584]{2,1,0:T(8,128)(2,1)} %param.10) | data formatting | bytes 1835008 | tf_op args[0]
  91.0 2.3 %copy.36 = bf16[128,8,448]{2,0,1:T(8,128)(2,1)} copy(bf16[128,8,448]{0,2,1:T(8,128)(2,1)} %bitcast.121) | data formatting | bytes 1835008 | tf_op jit(solution)/shard_map/reshape;squeeze | solution.py:285
  93.4 2.5 %maximum_maximum_fusion = bf16[8,128,512]{2,1,0:T(8,128)(2,1)} fusion(bf16[8,128,1]{2,1,0:T(8,128)(2,1)S(1)} %broadcast_in_dim.141, bf16[8,128,448]{2,1,0:T(8,128)(2,1)} %bitcast.118, bf16[512]{0:T(512)(128)(2,1)S(1)} %pad.2.clone), kind=kLoop, calls=%fused_computation.1 | loop fusion | flops 3145728 | bytes 1969152 | tf_op jit(solution)/shard_map/concatenate | solution.py:288
  96.0 5.0 %all-to-all-start = ((bf16[8,128,512]{2,1,0:T(8,128)(2,1)}), bf16[8,128,512]{2,1,0:T(8,128)(2,1)}, u32[]{:S(2)}, u32[]{:S(2)}) async-start(bf16[8,128,512]{2,1,0:T(8,128)(2,1)} %maximum_maximum_fusion), calls=%async_computation | async-start | bytes 2097152 | tf_op jit(solution)/shard_map/all_to_all | solution.py:289
  101.0 3.4 %shard_map.130 = (bf16[128,3584]{1,0:T(8,128)(2,1)}, bf16[128,3584]{1,0:T(8,128)(2,1)}, f32[1,512,256]{2,1,0:T(8,128)S(1)}) custom-call(s32[1]{0:T(128)} %get-tuple-element.33.heads_ref, bf16[128,3584]{1,0:T(8,128)(2,1)S(1)} %bitcast.108, bf16[128,3584]{1,0:T(8,128)(2,1)S(1)} %bitcast.111, ...), custom_call_target="tpu_custom_call", output_to_operand_aliasing={{0}: (6, {}), {1}: (7, {})} | custom-call | flops 822083584 | bytes 1703936 | tf_op jit(solution)/shard_map/pallas_call | solution.py:84
  104.5 1.5 collective-permute-start.19
  106.0 5.8 %shard_map.131 = (bf16[128,3584]{1,0:T(8,128)(2,1)}, bf16[128,3584]{1,0:T(8,128)(2,1)}, f32[2,512,256]{2,1,0:T(8,128)S(1)}) custom-call(s32[2]{0:T(128)S(1)} %bitcast.116, bf16[128,3584]{1,0:T(8,128)(2,1)S(1)} %bitcast.109, bf16[128,3584]{1,0:T(8,128)(2,1)S(1)} %bitcast.112, ...), custom_call_target="tpu_custom_call", output_to_operand_aliasing={{0}: (7, {}), {1}: (8, {})} | custom-call | flops 1644167168 | bytes 3407872 | tf_op jit(solution)/shard_map/pallas_call | solution.py:84
  112.1 6.7 %collective-permute-done.19 = f32[512,256]{1,0:T(8,128)S(1)} collective-permute-done((f32[512,256]{1,0:T(8,128)S(1)}, f32[512,256]{1,0:T(8,128)S(1)}, u32[]{:S(2)}, u32[]{:S(2)}) %collective-permute-start.19) | collective-permute-done | bytes 524320 | tf_op jit(solution)/shard_map/ppermute | solution.py:227
  119.1 2.1 %collective-permute-start.26 = (bf16[512,256]{1,0:T(8,128)(2,1)S(1)}, bf16[512,256]{1,0:T(8,128)(2,1)S(1)}, u32[]{:S(2)}, u32[]{:S(2)}) collective-permute-start(bf16[512,256]{1,0:T(8,128)(2,1)S(1)} %get-tuple-element.27.g_ref), channel_id=1, source_target_pairs={{0,8},{8,16},{16,24},{24,28},{28,20},{20,12},{12,4},{4,0},{1,9},{9... | collective-permute-start | bytes 786440 | tf_op jit(solution)/shard_map/ppermute | solution.py:247
  121.2 6.1 %all-to-all-done.refs_0_ = bf16[8,128,512]{2,1,0:T(8,128)(2,1)} async-done(((bf16[8,128,512]{2,1,0:T(8,128)(2,1)}), bf16[8,128,512]{2,1,0:T(8,128)(2,1)}, u32[]{:S(2)}, u32[]{:S(2)}) %all-to-all-start) | async-done | bytes 1048608 | tf_op jit(solution)/shard_map/all_to_all | solution.py:289
  127.3 1.4 collective-permute-start.24
  128.8 2.3 %collective-permute-start.27 = (bf16[512,256]{1,0:T(8,128)(2,1)S(1)}, bf16[512,256]{1,0:T(8,128)(2,1)S(1)}, u32[]{:S(2)}, u32[]{:S(2)}) collective-permute-start(bf16[512,256]{1,0:T(8,128)(2,1)S(1)} %get-tuple-element.27.g_ref), channel_id=1, source_target_pairs={{0,4},{8,0},{16,8},{24,16},{28,24},{20,28},{12,20},{4,12},{1,5},{9... | collective-permute-start | bytes 786440 | tf_op jit(solution)/shard_map/ppermute | solution.py:247
  131.5 4.5 %collective-permute-done.27.refs_0_ = bf16[512,256]{1,0:T(8,128)(2,1)S(1)} collective-permute-done((bf16[512,256]{1,0:T(8,128)(2,1)S(1)}, bf16[512,256]{1,0:T(8,128)(2,1)S(1)}, u32[]{:S(2)}, u32[]{:S(2)}) %collective-permute-start.27) | collective-permute-done | bytes 262176 | tf_op jit(solution)/shard_map/ppermute | solution.py:247
  136.0 7.4 %shard_map.132 = (f32[128,3584]{1,0:T(8,128)S(1)}, bf16[128,3584]{1,0:T(8,128)(2,1)S(1)}) custom-call(s32[2]{0:T(128)S(1)} %pad_add_fusion.1.quarters_ref, s32[512,1]{1,0:T(8,128)S(1)} %copy.34.kind_ref, bf16[512,256]{1,0:T(8,128)(2,1)S(1)} %get-tuple-element.27.g_ref, bf16[512,256]{1,0:T(8,128)(2,1)S(1)} %collective-permute-done.20.gc_ref, ...), custom_call_target="tpu_custom_call" | custom-call | flops 1879048192 | bytes 10092544 | tf_op jit(solution)/shard_map/pallas_call | solution.py:151
  143.5 0.9 copy-done
  144.4 1.3 copy-done.1
  145.7 2.0 %collective-permute-start.29 = (bf16[512,256]{1,0:T(8,128)(2,1)}, bf16[512,256]{1,0:T(8,128)(2,1)S(1)}, u32[]{:S(2)}, u32[]{:S(2)}) collective-permute-start(bf16[512,256]{1,0:T(8,128)(2,1)} %shard_map.134), channel_id=1, source_target_pairs={{0,4},{8,0},{16,8},{24,16},{28,24},{20,28},{12,20},{4,12},{1,5},{9... | collective-permute-start | bytes 786440 | tf_op jit(solution)/shard_map/ppermute | solution.py:247
  147.7 4.3 %collective-permute-done.24.refs_2_ = bf16[8,128,512]{2,1,0:T(8,128)(2,1)} collective-permute-done((bf16[8,128,512]{2,1,0:T(8,128)(2,1)}, bf16[8,128,512]{2,1,0:T(8,128)(2,1)}, u32[]{:S(2)}, u32[]{:S(2)}) %collective-permute-start.24) | collective-permute-done | bytes 1048608 | tf_op jit(solution)/shard_map/ppermute | solution.py:227
  152.0 1.4 collective-permute-start.22
  153.4 2.0 %collective-permute-start.31 = (bf16[512,256]{1,0:T(8,128)(2,1)S(1)}, bf16[512,256]{1,0:T(8,128)(2,1)S(1)}, u32[]{:S(2)}, u32[]{:S(2)}) collective-permute-start(bf16[512,256]{1,0:T(8,128)(2,1)S(1)} %collective-permute-done.29), channel_id=1, source_target_pairs={{0,4},{8,0},{16,8},{24,16},{28,24},{20,28},{12,20},{4,12},{1,5},{9... | collective-permute-start | bytes 786440 | tf_op jit(solution)/shard_map/ppermute | solution.py:247
  155.5 6.4 %collective-permute-done.30 = bf16[512,256]{1,0:T(8,128)(2,1)S(1)} collective-permute-done((bf16[512,256]{1,0:T(8,128)(2,1)S(1)}, bf16[512,256]{1,0:T(8,128)(2,1)S(1)}, u32[]{:S(2)}, u32[]{:S(2)}) %collective-permute-start.30) | collective-permute-done | bytes 262176 | tf_op jit(solution)/shard_map/ppermute | solution.py:247
  162.2 1.8 %collective-permute-start.33 = (bf16[256,256]{1,0:T(8,128)(2,1)S(1)}, bf16[256,256]{1,0:T(8,128)(2,1)S(1)}, u32[]{:S(2)}, u32[]{:S(2)}) collective-permute-start(bf16[256,256]{1,0:T(8,128)(2,1)S(1)} %slice.67), channel_id=1, source_target_pairs={{0,4},{8,0},{16,8},{24,16},{28,24},{20,28},{12,20},{4,12},{1,5},{9... | collective-permute-start | bytes 393224 | tf_op jit(solution)/shard_map/ppermute | solution.py:247
  164.0 2.8 %collective-permute-done.32 = bf16[256,256]{1,0:T(8,128)(2,1)S(1)} collective-permute-done((bf16[256,256]{1,0:T(8,128)(2,1)S(1)}, bf16[256,256]{1,0:T(8,128)(2,1)S(1)}, u32[]{:S(2)}, u32[]{:S(2)}) %collective-permute-start.32) | collective-permute-done | bytes 131104 | tf_op jit(solution)/shard_map/ppermute | solution.py:247
  167.3 8.0 %shard_map.135 = f32[2,448,256]{2,1,0:T(8,128)} custom-call(s32[4]{0:T(128)S(1)} %iota_xor_fusion.quarters_ref, bf16[8,128,512]{2,1,0:T(8,128)(2,1)} %all-to-all-done.refs_0_, bf16[8,128,512]{2,1,0:T(8,128)(2,1)S(1)} %collective-permute-done.23.refs_1_, bf16[8,128,512]{2,1,0:T(8,128)(2,1)} %collective-permute-done.24.refs_2_, ...), custom_call_target="tpu_custom_call" | custom-call | flops 2147483648 | bytes 7208960 | tf_op jit(solution)/shard_map/pallas_call | solution.py:198
  175.3 1.1 fusion
  (111 shorter events, 13.8 us)
Async XLA Ops:
  0.6 9.8 %copy-start.5 = (bf16[1,128,3584]{2,1,0:T(8,128)(2,1)S(1)}, bf16[1,128,3584]{2,1,0:T(8,128)(2,1)}, u32[]{:S(2)}) copy-start(bf16[1,128,3584]{2,1,0:T(8,128)(2,1)} %param.10) | copy-start | bytes 2752516
  0.6 10.8 %copy-start.11 = (s32[8]{0:T(128)S(1)}, s32[8]{0:T(128)}, u32[]{:S(2)}) copy-start(s32[8]{0:T(128)} %constant.135.clone) | copy-start | bytes 100
  0.7 39.9 %collective-permute-start.3 = (bf16[128,3584]{1,0:T(8,128)(2,1)}, bf16[128,3584]{1,0:T(8,128)(2,1)S(1)}, u32[]{:S(2)}, u32[]{:S(2)}) collective-permute-start(bf16[128,3584]{1,0:T(8,128)(2,1)} %bitcast.119), channel_id=1, source_target_pairs={{0,1},{1,0},{2,3},{3,2},{4,5},{5,4},{6,7},{7,6},{8,9},{9,8},{10,11... | collective-permute-start | bytes 2752520 | tf_op jit(solution)/shard_map/ppermute | solution.py:227
  1.2 39.4 %collective-permute-start.4 = (bf16[128,3584]{1,0:T(8,128)(2,1)}, bf16[128,3584]{1,0:T(8,128)(2,1)S(1)}, u32[]{:S(2)}, u32[]{:S(2)}) collective-permute-start(bf16[128,3584]{1,0:T(8,128)(2,1)} %bitcast.120), channel_id=1, source_target_pairs={{0,2},{1,3},{2,0},{3,1},{4,6},{5,7},{6,4},{7,5},{8,10},{9,11},{10,... | collective-permute-start | bytes 2752520 | tf_op jit(solution)/shard_map/ppermute | solution.py:227
  5.7 29.1 %collective-permute-start.6 = (bf16[448,512]{1,0:T(8,128)(2,1)}, bf16[448,512]{1,0:T(8,128)(2,1)}, u32[]{:S(2)}, u32[]{:S(2)}) collective-permute-start(bf16[448,512]{1,0:T(8,128)(2,1)} %pad_maximum_fusion), channel_id=1, source_target_pairs={{0,8},{8,16},{16,24},{24,28},{28,20},{20,12},{12,4},{4,0},{1,9},{9... | collective-permute-start | bytes 1376264 | tf_op jit(solution)/shard_map/ppermute | solution.py:247
  7.2 29.4 %collective-permute-start.7 = (bf16[448,512]{1,0:T(8,128)(2,1)}, bf16[448,512]{1,0:T(8,128)(2,1)}, u32[]{:S(2)}, u32[]{:S(2)}) collective-permute-start(bf16[448,512]{1,0:T(8,128)(2,1)} %pad_maximum_fusion), channel_id=1, source_target_pairs={{0,4},{8,0},{16,8},{24,16},{28,24},{20,28},{12,20},{4,12},{1,5},{9... | collective-permute-start | bytes 1376264 | tf_op jit(solution)/shard_map/ppermute | solution.py:247
  8.4 13.4 %collective-permute-start = (s32[2,128]{1,0:T(2,128)S(1)}, s32[2,128]{1,0:T(2,128)S(1)}, u32[]{:S(2)}, u32[]{:S(2)}) collective-permute-start(s32[2,128]{1,0:T(2,128)S(1)} %pad_add_fusion), channel_id=1, source_target_pairs={{0,1},{1,0},{2,3},{3,2},{4,5},{5,4},{6,7},{7,6},{8,9},{9,8},{10,11... | collective-permute-start | bytes 3080 | tf_op jit(solution)/shard_map/ppermute | solution.py:227
  10.4 9.3 %copy-start.8 = (s32[8]{0:T(128)S(1)}, s32[8]{0:T(128)}, u32[]{:S(2)}) copy-start(s32[8]{0:T(128)} %constant.134.clone) | copy-start | bytes 100
  21.8 6.6 %collective-permute-start.1 = (s32[2,128]{1,0:T(2,128)S(1)}, s32[2,128]{1,0:T(2,128)S(1)}, u32[]{:S(2)}, u32[]{:S(2)}) collective-permute-start(s32[2,128]{1,0:T(2,128)S(1)} %pad_add_fusion), channel_id=1, source_target_pairs={{0,2},{1,3},{2,0},{3,1},{4,6},{5,7},{6,4},{7,5},{8,10},{9,11},{10,... | collective-permute-start | bytes 3080 | tf_op jit(solution)/shard_map/ppermute | solution.py:227
  28.3 6.4 %collective-permute-start.2 = (s32[2,128]{1,0:T(2,128)S(1)}, s32[2,128]{1,0:T(2,128)S(1)}, u32[]{:S(2)}, u32[]{:S(2)}) collective-permute-start(s32[2,128]{1,0:T(2,128)S(1)} %collective-permute-done.1), channel_id=1, source_target_pairs={{0,1},{1,0},{2,3},{3,2},{4,5},{5,4},{6,7},{7,6},{8,9},{9,8},{10,11... | collective-permute-start | bytes 3080 | tf_op jit(solution)/shard_map/ppermute | solution.py:227
  34.8 12.9 %collective-permute-start.8 = (bf16[448,512]{1,0:T(8,128)(2,1)}, bf16[448,512]{1,0:T(8,128)(2,1)S(1)}, u32[]{:S(2)}, u32[]{:S(2)}) collective-permute-start(bf16[448,512]{1,0:T(8,128)(2,1)} %collective-permute-done.6), channel_id=1, source_target_pairs={{0,8},{8,16},{16,24},{24,28},{28,20},{20,12},{12,4},{4,0},{1,9},{9... | collective-permute-start | bytes 1376264 | tf_op jit(solution)/shard_map/ppermute | solution.py:247
  36.6 12.9 %collective-permute-start.9 = (bf16[448,512]{1,0:T(8,128)(2,1)}, bf16[448,512]{1,0:T(8,128)(2,1)S(1)}, u32[]{:S(2)}, u32[]{:S(2)}) collective-permute-start(bf16[448,512]{1,0:T(8,128)(2,1)} %collective-permute-done.7), channel_id=1, source_target_pairs={{0,4},{8,0},{16,8},{24,16},{28,24},{20,28},{12,20},{4,12},{1,5},{9... | collective-permute-start | bytes 1376264 | tf_op jit(solution)/shard_map/ppermute | solution.py:247
  40.6 27.8 %collective-permute-start.5 = (bf16[128,3584]{1,0:T(8,128)(2,1)S(1)}, bf16[128,3584]{1,0:T(8,128)(2,1)S(1)}, u32[]{:S(2)}, u32[]{:S(2)}) collective-permute-start(bf16[128,3584]{1,0:T(8,128)(2,1)S(1)} %collective-permute-done.4), channel_id=1, source_target_pairs={{0,1},{1,0},{2,3},{3,2},{4,5},{5,4},{6,7},{7,6},{8,9},{9,8},{10,11... | collective-permute-start | bytes 2752520 | tf_op jit(solution)/shard_map/ppermute | solution.py:227
  47.7 11.9 %collective-permute-start.10 = (bf16[448,512]{1,0:T(8,128)(2,1)S(1)}, bf16[448,512]{1,0:T(8,128)(2,1)S(1)}, u32[]{:S(2)}, u32[]{:S(2)}) collective-permute-start(bf16[448,512]{1,0:T(8,128)(2,1)S(1)} %collective-permute-done.8), channel_id=1, source_target_pairs={{0,8},{8,16},{16,24},{24,28},{28,20},{20,12},{12,4},{4,0},{1,9},{9... | collective-permute-start | bytes 1376264 | tf_op jit(solution)/shard_map/ppermute | solution.py:247
  49.6 12.0 %collective-permute-start.11 = (bf16[448,512]{1,0:T(8,128)(2,1)S(1)}, bf16[448,512]{1,0:T(8,128)(2,1)S(1)}, u32[]{:S(2)}, u32[]{:S(2)}) collective-permute-start(bf16[448,512]{1,0:T(8,128)(2,1)S(1)} %collective-permute-done.9), channel_id=1, source_target_pairs={{0,4},{8,0},{16,8},{24,16},{28,24},{20,28},{12,20},{4,12},{1,5},{9... | collective-permute-start | bytes 1376264 | tf_op jit(solution)/shard_map/ppermute | solution.py:247
  59.7 6.1 %collective-permute-start.12 = (bf16[224,512]{1,0:T(8,128)(2,1)S(1)}, bf16[224,512]{1,0:T(8,128)(2,1)S(1)}, u32[]{:S(2)}, u32[]{:S(2)}) collective-permute-start(bf16[224,512]{1,0:T(8,128)(2,1)S(1)} %slice.61), channel_id=1, source_target_pairs={{0,8},{8,16},{16,24},{24,28},{28,20},{20,12},{12,4},{4,0},{1,9},{9... | collective-permute-start | bytes 688136 | tf_op jit(solution)/shard_map/ppermute | solution.py:247
  61.6 6.1 %collective-permute-start.13 = (bf16[224,512]{1,0:T(8,128)(2,1)S(1)}, bf16[224,512]{1,0:T(8,128)(2,1)S(1)}, u32[]{:S(2)}, u32[]{:S(2)}) collective-permute-start(bf16[224,512]{1,0:T(8,128)(2,1)S(1)} %slice.62), channel_id=1, source_target_pairs={{0,4},{8,0},{16,8},{24,16},{28,24},{20,28},{12,20},{4,12},{1,5},{9... | collective-permute-start | bytes 688136 | tf_op jit(solution)/shard_map/ppermute | solution.py:247
  68.4 67.6 %collective-permute-start.21 = (bf16[3584,512]{1,0:T(8,128)(2,1)}, bf16[3584,512]{1,0:T(8,128)(2,1)}, u32[]{:S(2)}, u32[]{:S(2)}) collective-permute-start(bf16[3584,512]{1,0:T(8,128)(2,1)} %bitcast.41.w_ref), channel_id=1, source_target_pairs={{0,1},{1,0},{2,3},{3,2},{4,5},{5,4},{6,7},{7,6},{8,9},{9,8},{10,11... | collective-permute-start | bytes 11010056 | tf_op jit(solution)/shard_map/ppermute | solution.py:227
  69.4 14.9 %copy-start.9 = (s32[1,128]{1,0:T(1,128)S(1)}, s32[1,128]{1,0:T(1,128)}, u32[]{:S(2)}) copy-start(s32[1,128]{1,0:T(1,128)} %param.14) | copy-start | bytes 1540
  69.4 15.8 %copy-start.3 = (bf16[1,128,3584]{2,1,0:T(8,128)(2,1)S(1)}, bf16[1,128,3584]{2,1,0:T(8,128)(2,1)}, u32[]{:S(2)}) copy-start(bf16[1,128,3584]{2,1,0:T(8,128)(2,1)} %param.11) | copy-start | bytes 2752516
  69.4 15.8 %copy-start.4 = (bf16[1,128,3584]{2,1,0:T(8,128)(2,1)S(1)}, bf16[1,128,3584]{2,1,0:T(8,128)(2,1)}, u32[]{:S(2)}) copy-start(bf16[1,128,3584]{2,1,0:T(8,128)(2,1)} %param.12) | copy-start | bytes 2752516
  74.7 14.1 %copy-start.10 = (s32[1,128]{1,0:T(1,128)S(1)}, s32[1,128]{1,0:T(1,128)}, u32[]{:S(2)}) copy-start(s32[1,128]{1,0:T(1,128)} %param.13) | copy-start | bytes 1540
  74.9 8.8 %collective-permute-start.15 = (bf16[512,256]{1,0:T(8,128)(2,1)S(1)}, bf16[512,256]{1,0:T(8,128)(2,1)S(1)}, u32[]{:S(2)}, u32[]{:S(2)}) collective-permute-start(bf16[512,256]{1,0:T(8,128)(2,1)S(1)} %fusion.1.refs_0_), channel_id=1, source_target_pairs={{0,2},{1,3},{2,0},{3,1},{4,6},{5,7},{6,4},{7,5},{8,10},{9,11},{10,... | collective-permute-start | bytes 786440 | tf_op jit(solution)/shard_map/ppermute | solution.py:227
  83.7 1.5 collective-permute-start.16
  88.6 15.8 %collective-permute-start.17 = (f32[512,256]{1,0:T(8,128)S(1)}, f32[512,256]{1,0:T(8,128)S(1)}, u32[]{:S(2)}, u32[]{:S(2)}) collective-permute-start(f32[512,256]{1,0:T(8,128)S(1)} %bitcast.117), channel_id=1, source_target_pairs={{0,1},{1,0},{2,3},{3,2},{4,5},{5,4},{6,7},{7,6},{8,9},{9,8},{10,11... | collective-permute-start | bytes 1572872 | tf_op jit(solution)/shard_map/ppermute | solution.py:227
  96.0 31.4 %all-to-all-start = ((bf16[8,128,512]{2,1,0:T(8,128)(2,1)}), bf16[8,128,512]{2,1,0:T(8,128)(2,1)}, u32[]{:S(2)}, u32[]{:S(2)}) async-start(bf16[8,128,512]{2,1,0:T(8,128)(2,1)} %maximum_maximum_fusion), calls=%async_computation | async-start | bytes 2097152 | tf_op jit(solution)/shard_map/all_to_all | solution.py:289
  100.9 5.1 %collective-permute-start.14 = (bf16[512,256]{1,0:T(8,128)(2,1)S(1)}, bf16[512,256]{1,0:T(8,128)(2,1)S(1)}, u32[]{:S(2)}, u32[]{:S(2)}) collective-permute-start(bf16[512,256]{1,0:T(8,128)(2,1)S(1)} %fusion.1.refs_0_), channel_id=1, source_target_pairs={{0,1},{1,0},{2,3},{3,2},{4,5},{5,4},{6,7},{7,6},{8,9},{9,8},{10,11... | collective-permute-start | bytes 786440 | tf_op jit(solution)/shard_map/ppermute | solution.py:227
  104.5 14.3 %collective-permute-start.19 = (f32[512,256]{1,0:T(8,128)S(1)}, f32[512,256]{1,0:T(8,128)S(1)}, u32[]{:S(2)}, u32[]{:S(2)}) collective-permute-start(f32[512,256]{1,0:T(8,128)S(1)} %bitcast_add_fusion.1.refs_6_), channel_id=1, source_target_pairs={{0,2},{1,3},{2,0},{3,1},{4,6},{5,7},{6,4},{7,5},{8,10},{9,11},{10,... | collective-permute-start | bytes 1572872 | tf_op jit(solution)/shard_map/ppermute | solution.py:227
  111.9 6.9 %collective-permute-start.18 = (f32[512,256]{1,0:T(8,128)S(1)}, f32[512,256]{1,0:T(8,128)S(1)}, u32[]{:S(2)}, u32[]{:S(2)}) collective-permute-start(f32[512,256]{1,0:T(8,128)S(1)} %slice_bitcast_fusion), channel_id=1, source_target_pairs={{0,1},{1,0},{2,3},{3,2},{4,5},{5,4},{6,7},{7,6},{8,9},{9,8},{10,11... | collective-permute-start | bytes 1572872 | tf_op jit(solution)/shard_map/ppermute | solution.py:227
  119.1 12.3 %collective-permute-start.26 = (bf16[512,256]{1,0:T(8,128)(2,1)S(1)}, bf16[512,256]{1,0:T(8,128)(2,1)S(1)}, u32[]{:S(2)}, u32[]{:S(2)}) collective-permute-start(bf16[512,256]{1,0:T(8,128)(2,1)S(1)} %get-tuple-element.27.g_ref), channel_id=1, source_target_pairs={{0,8},{8,16},{16,24},{24,28},{28,20},{20,12},{12,4},{4,0},{1,9},{9... | collective-permute-start | bytes 786440 | tf_op jit(solution)/shard_map/ppermute | solution.py:247
  127.3 24.6 %collective-permute-start.24 = (bf16[8,128,512]{2,1,0:T(8,128)(2,1)}, bf16[8,128,512]{2,1,0:T(8,128)(2,1)}, u32[]{:S(2)}, u32[]{:S(2)}) collective-permute-start(bf16[8,128,512]{2,1,0:T(8,128)(2,1)} %all-to-all-done.refs_0_), channel_id=1, source_target_pairs={{0,2},{1,3},{2,0},{3,1},{4,6},{5,7},{6,4},{7,5},{8,10},{9,11},{10,... | collective-permute-start | bytes 3145736 | tf_op jit(solution)/shard_map/ppermute | solution.py:227
  128.8 7.2 %collective-permute-start.27 = (bf16[512,256]{1,0:T(8,128)(2,1)S(1)}, bf16[512,256]{1,0:T(8,128)(2,1)S(1)}, u32[]{:S(2)}, u32[]{:S(2)}) collective-permute-start(bf16[512,256]{1,0:T(8,128)(2,1)S(1)} %get-tuple-element.27.g_ref), channel_id=1, source_target_pairs={{0,4},{8,0},{16,8},{24,16},{28,24},{20,28},{12,20},{4,12},{1,5},{9... | collective-permute-start | bytes 786440 | tf_op jit(solution)/shard_map/ppermute | solution.py:247
  131.3 4.6 %collective-permute-start.20 = (bf16[512,256]{1,0:T(8,128)(2,1)S(1)}, bf16[512,256]{1,0:T(8,128)(2,1)S(1)}, u32[]{:S(2)}, u32[]{:S(2)}) collective-permute-start(bf16[512,256]{1,0:T(8,128)(2,1)S(1)} %get-tuple-element.27.g_ref), channel_id=1, source_target_pairs={{0,1},{1,0},{2,3},{3,2},{4,5},{5,4},{6,7},{7,6},{8,9},{9,8},{10,11... | collective-permute-start | bytes 786440 | tf_op jit(solution)/shard_map/ppermute | solution.py:227
  131.4 12.0 %copy-start.6 = (bf16[512,256]{1,0:T(8,128)(2,1)}, bf16[512,256]{1,0:T(8,128)(2,1)S(1)}, u32[]{:S(2)}) copy-start(bf16[512,256]{1,0:T(8,128)(2,1)S(1)} %collective-permute-done.26.refs_0_) | copy-start | bytes 786436
  135.9 7.5 %copy-start.7 = (bf16[512,256]{1,0:T(8,128)(2,1)}, bf16[512,256]{1,0:T(8,128)(2,1)S(1)}, u32[]{:S(2)}) copy-start(bf16[512,256]{1,0:T(8,128)(2,1)S(1)} %collective-permute-done.27.refs_0_) | copy-start | bytes 786436
  143.4 0.9 copy-start
  144.4 1.3 copy-start.1
  145.7 7.7 %collective-permute-start.28 = (bf16[512,256]{1,0:T(8,128)(2,1)}, bf16[512,256]{1,0:T(8,128)(2,1)S(1)}, u32[]{:S(2)}, u32[]{:S(2)}) collective-permute-start(bf16[512,256]{1,0:T(8,128)(2,1)} %shard_map.133), channel_id=1, source_target_pairs={{0,8},{8,16},{16,24},{24,28},{28,20},{20,12},{12,4},{4,0},{1,9},{9... | collective-permute-start | bytes 786440 | tf_op jit(solution)/shard_map/ppermute | solution.py:247
  145.7 7.8 %collective-permute-start.29 = (bf16[512,256]{1,0:T(8,128)(2,1)}, bf16[512,256]{1,0:T(8,128)(2,1)S(1)}, u32[]{:S(2)}, u32[]{:S(2)}) collective-permute-start(bf16[512,256]{1,0:T(8,128)(2,1)} %shard_map.134), channel_id=1, source_target_pairs={{0,4},{8,0},{16,8},{24,16},{28,24},{20,28},{12,20},{4,12},{1,5},{9... | collective-permute-start | bytes 786440 | tf_op jit(solution)/shard_map/ppermute | solution.py:247
  147.7 19.6 %collective-permute-start.23 = (bf16[8,128,512]{2,1,0:T(8,128)(2,1)}, bf16[8,128,512]{2,1,0:T(8,128)(2,1)S(1)}, u32[]{:S(2)}, u32[]{:S(2)}) collective-permute-start(bf16[8,128,512]{2,1,0:T(8,128)(2,1)} %all-to-all-done.refs_0_), channel_id=1, source_target_pairs={{0,1},{1,0},{2,3},{3,2},{4,5},{5,4},{6,7},{7,6},{8,9},{9,8},{10,11... | collective-permute-start | bytes 3145736 | tf_op jit(solution)/shard_map/ppermute | solution.py:227
  152.0 15.3 %collective-permute-start.25 = (bf16[8,128,512]{2,1,0:T(8,128)(2,1)}, bf16[8,128,512]{2,1,0:T(8,128)(2,1)S(1)}, u32[]{:S(2)}, u32[]{:S(2)}) collective-permute-start(bf16[8,128,512]{2,1,0:T(8,128)(2,1)} %collective-permute-done.24.refs_2_), channel_id=1, source_target_pairs={{0,1},{1,0},{2,3},{3,2},{4,5},{5,4},{6,7},{7,6},{8,9},{9,8},{10,11... | collective-permute-start | bytes 3145736 | tf_op jit(solution)/shard_map/ppermute | solution.py:227
  152.0 23.3 %collective-permute-start.22 = (bf16[128,3584]{1,0:T(8,128)(2,1)}, bf16[128,3584]{1,0:T(8,128)(2,1)S(1)}, u32[]{:S(2)}, u32[]{:S(2)}) collective-permute-start(bf16[128,3584]{1,0:T(8,128)(2,1)} %copy-done), channel_id=1, source_target_pairs={{0,2},{1,3},{2,0},{3,1},{4,6},{5,7},{6,4},{7,5},{8,10},{9,11},{10,... | collective-permute-start | bytes 2752520 | tf_op jit(solution)/shard_map/ppermute | solution.py:227
  153.4 8.4 %collective-permute-start.30 = (bf16[512,256]{1,0:T(8,128)(2,1)S(1)}, bf16[512,256]{1,0:T(8,128)(2,1)S(1)}, u32[]{:S(2)}, u32[]{:S(2)}) collective-permute-start(bf16[512,256]{1,0:T(8,128)(2,1)S(1)} %collective-permute-done.28), channel_id=1, source_target_pairs={{0,8},{8,16},{16,24},{24,28},{28,20},{20,12},{12,4},{4,0},{1,9},{9... | collective-permute-start | bytes 786440 | tf_op jit(solution)/shard_map/ppermute | solution.py:247
  153.4 8.8 %collective-permute-start.31 = (bf16[512,256]{1,0:T(8,128)(2,1)S(1)}, bf16[512,256]{1,0:T(8,128)(2,1)S(1)}, u32[]{:S(2)}, u32[]{:S(2)}) collective-permute-start(bf16[512,256]{1,0:T(8,128)(2,1)S(1)} %collective-permute-done.29), channel_id=1, source_target_pairs={{0,4},{8,0},{16,8},{24,16},{28,24},{20,28},{12,20},{4,12},{1,5},{9... | collective-permute-start | bytes 786440 | tf_op jit(solution)/shard_map/ppermute | solution.py:247
  161.8 5.0 %collective-permute-start.32 = (bf16[256,256]{1,0:T(8,128)(2,1)S(1)}, bf16[256,256]{1,0:T(8,128)(2,1)S(1)}, u32[]{:S(2)}, u32[]{:S(2)}) collective-permute-start(bf16[256,256]{1,0:T(8,128)(2,1)S(1)} %slice.66), channel_id=1, source_target_pairs={{0,8},{8,16},{16,24},{24,28},{28,20},{20,12},{12,4},{4,0},{1,9},{9... | collective-permute-start | bytes 393224 | tf_op jit(solution)/shard_map/ppermute | solution.py:247
  162.2 5.0 %collective-permute-start.33 = (bf16[256,256]{1,0:T(8,128)(2,1)S(1)}, bf16[256,256]{1,0:T(8,128)(2,1)S(1)}, u32[]{:S(2)}, u32[]{:S(2)}) collective-permute-start(bf16[256,256]{1,0:T(8,128)(2,1)S(1)} %slice.67), channel_id=1, source_target_pairs={{0,4},{8,0},{16,8},{24,16},{28,24},{20,28},{12,20},{4,12},{1,5},{9... | collective-permute-start | bytes 393224 | tf_op jit(solution)/shard_map/ppermute | solution.py:247
  167.2 8.0 %copy-start.2 = (f32[128,3584]{1,0:T(8,128)S(1)}, f32[128,3584]{1,0:T(8,128)}, u32[]{:S(2)}) copy-start(f32[128,3584]{1,0:T(8,128)} %copy-done.1) | copy-start | bytes 5505028
